TPU v7x, 512 devices: a whole 4x8x8 slice. The times are simulated.
512 devices in a mesh: patch: 64 (over z, x, core), head: 4 (over y_hi), cfg: 2 (over y_lo).
Axes of the slice: x: 4, y: 8 (y_hi: 4, y_lo: 2; y = y_hi * 2 + y_lo), z: 8, core: 2. Of those that a mesh axis runs over, the one named last changes fastest.
Arguments:
- tokens: bfloat16 [16384, 1280], P(('cfg', 'patch')), parts along dimension 0, may hold values from -230 to 230, as said below
- norm_gain: float32 [1280], replicated, may hold values from 0.1 to 1.9
- norm_bias: float32 [1280], replicated, may hold values from -3 to 3
- w_query: bfloat16 [1280, 1024], P(None, 'head'), may hold values from -0.15625 to 0.15625
- w_key: bfloat16 [1280, 1024], P(None, 'head'), may hold values from -0.625 to 0.625
- w_value: bfloat16 [1280, 1024], P(None, 'head'), may hold values from -0.15625 to 0.15625
- w_out: bfloat16 [1024, 1280], P('head'), may hold values from -0.75 to 0.75
- stale_keys: bfloat16 [16384, 1024], P(('cfg', 'patch'), 'head'), parts along dimension 0, may hold values from -340 to 340, as said below
- stale_values: bfloat16 [16384, 1024], P(('cfg', 'patch'), 'head'), parts along dimension 0, may hold values from -6 to 6
Outputs:
- mixed: bfloat16 [16384, 1280], P(('cfg', 'patch'), 'head'), parts along dimension 0
There are 2 independent parts, one for each index of `cfg`. A program takes and returns all parts, laid end to end along the dimension named above; an argument that names none is the same for every part. Nothing has to cross between parts.
Inputs may be any that keep to these rules, and one draw needn't show every extreme that they name: `tokens`: Real-valued activations of order one to a few tens. `stale_keys`: Real-valued keys.
All inputs are finite; a program needn't handle non-finite values.
Results may differ from a plain program's by a relative error of at most 0.015.
The roundings to bfloat16 on the way count: a program that leaves them out, or rounds other values in their place, can miss the bound.
Values may be sent and summed in bfloat16 or wider, within the bound.
A program may use at most 64 MiB of HBM per device.

v0:
```python
import math

import jax
import jax.numpy as jnp
from jax import lax
from jax.sharding import PartitionSpec as P

HEAD_DIM = 64
GROUPS = 32


epsilon = 1e-06


def attend(state, pieces, queries, own_start, own_rows):
    keys_piece, values_piece = pieces
    length = keys_piece.shape[0]
    width = math.gcd(length, 2048)
    heads = queries.shape[1]

    def one_block(index, carry):
        top, total, summed = carry
        offset = index * width
        keys_block = lax.dynamic_slice_in_dim(keys_piece, offset, width, 0).reshape(
            width, heads, HEAD_DIM
        )
        values_block = lax.dynamic_slice_in_dim(values_piece, offset, width, 0).reshape(
            width, heads, HEAD_DIM
        )
        scores = (
            jnp.einsum("qhd,khd->qhk", queries, keys_block, preferred_element_type=jnp.float32)
            * 0.125
        )
        intersections = (offset < own_start + own_rows) & (offset + width > own_start)

        def masked(values_in):
            position = offset + jnp.arange(width, dtype=jnp.int32)
            inside = (position >= own_start) & (position < own_start + own_rows)
            return jnp.where(inside[None, None, :], -jnp.inf, values_in)

        scores = lax.cond(intersections, masked, lambda values_in: values_in, scores)
        new_top = jnp.maximum(top, jnp.max(scores, axis=2))
        factor = jnp.exp(top - new_top)
        weights = jnp.exp(scores - new_top[..., None])
        total = total * factor + jnp.sum(weights, axis=2)
        summed = summed * factor[..., None] + jnp.einsum(
            "qhk,khd->qhd",
            weights.astype(jnp.bfloat16),
            values_block,
            preferred_element_type=jnp.float32,
        )
        return (new_top, total, summed)

    return lax.fori_loop(0, length // width, one_block, state)


def per_device(
    tokens, norm_gain, norm_bias, w_query, w_key, w_value, w_out, stale_keys, stale_values
):
    tok_dev, channels = tokens.shape
    inner_dev = w_query.shape[1]
    heads = inner_dev // HEAD_DIM
    grouped = tokens.astype(jnp.float32).reshape(tok_dev, GROUPS, channels // GROUPS)
    count = tok_dev * lax.axis_size("patch") * (channels // GROUPS)
    group_total = lax.psum(jnp.sum(grouped, axis=(0, 2)), "patch")
    group_mean = group_total / count
    centered = grouped - group_mean[None, :, None]
    squares = lax.psum(jnp.sum(centered * centered, axis=(0, 2)), "patch")
    group_var = squares / count
    normed = (centered * lax.rsqrt(group_var + epsilon)[None, :, None]).reshape(tok_dev, channels)
    normed = (normed * norm_gain + norm_bias).astype(jnp.bfloat16)
    query = jnp.dot(normed, w_query, preferred_element_type=jnp.float32).astype(jnp.bfloat16)
    fresh_keys = jnp.dot(normed, w_key, preferred_element_type=jnp.float32).astype(jnp.bfloat16)
    fresh_values = jnp.dot(normed, w_value, preferred_element_type=jnp.float32).astype(jnp.bfloat16)
    queries = query.reshape(tok_dev, heads, HEAD_DIM)
    own_keys = fresh_keys.reshape(tok_dev, heads, HEAD_DIM)
    own_values = fresh_values.reshape(tok_dev, heads, HEAD_DIM)
    own_scores = (
        jnp.einsum("qhd,khd->qhk", queries, own_keys, preferred_element_type=jnp.float32) * 0.125
    )
    top = jnp.max(own_scores, axis=2)
    own_weights = jnp.exp(own_scores - top[..., None])
    total = jnp.sum(own_weights, axis=2)
    summed = jnp.einsum(
        "qhk,khd->qhd",
        own_weights.astype(jnp.bfloat16),
        own_values,
        preferred_element_type=jnp.float32,
    )
    own_start = lax.axis_index("patch") * tok_dev
    top, total, summed = attend(
        (top, total, summed),
        (
            lax.all_gather(stale_keys, "patch", axis=0, tiled=True),
            lax.all_gather(stale_values, "patch", axis=0, tiled=True),
        ),
        queries,
        own_start,
        tok_dev,
    )
    attended = (summed / total[..., None]).reshape(tok_dev, inner_dev).astype(jnp.bfloat16)
    partial_out = jnp.dot(attended, w_out, preferred_element_type=jnp.float32)
    mixed = lax.psum_scatter(
        partial_out.astype(jnp.bfloat16), "head", scatter_dimension=1, tiled=True
    )
    return mixed


def solution(mesh):
    in_specs = (
        P(("cfg", "patch"), None),
        P(),
        P(),
        P(None, "head"),
        P(None, "head"),
        P(None, "head"),
        P("head", None),
        P(("cfg", "patch"), "head"),
        P(("cfg", "patch"), "head"),
    )
    out_specs = P(("cfg", "patch"), "head")
    return jax.shard_map(
        per_device, mesh=mesh, in_specs=in_specs, out_specs=out_specs, check_vma=False
    )
```

profile of v0, /device:TPU:6, one launch (start us, length us, event | category | flops | bytes accessed | tf_op | source)
XLA Modules:
  0.0 393.2 jit_solution(5029092480422351230)
XLA Ops:
  11.2 120.1 %psum.14 = f32[32]{0:T(128)S(1)} all-reduce(f32[32]{0:T(128)S(1)} %reduce_sum.57), channel_id=1, replica_groups=mesh['patch'=64,'head'=4,'cfg'=2] {'patch'}, use_global_device_ids=true, to_apply=%region_2.0 | all-reduce | flops 32 | bytes 256 | tf_op jit(solution)/shard_map/psum | solution.py:65
  132.8 124.4 %psum.15 = f32[32]{0:T(128)S(1)} all-reduce(f32[32]{0:T(128)S(1)} %reduce_sum.60), channel_id=1, replica_groups=mesh['patch'=64,'head'=4,'cfg'=2] {'patch'}, use_global_device_ids=true, to_apply=%region_5.0 | all-reduce | flops 32 | bytes 256 | tf_op jit(solution)/shard_map/psum | solution.py:68
  261.8 86.9 %while.18 = (s32[]{:T(128)}, f32[128,4]{1,0:T(8,128)S(1)}, f32[128,4]{1,0:T(8,128)S(1)}, f32[128,4,64]{0,2,1:T(8,128)S(1)}, s32[]{:T(128)}, /*index=5*/s32[]{:T(...) while((s32[]{:T(128)}, f32[128,4]{1,0:T(8,128)S(1)}, ...), condition=%wide.region_14.15_spmd, body=%wide.region_8.14_spmd.sunk | while | flops 274801664 | bytes 36018460 | solution.py:54
  261.8 2.7 constant_dynamic-slice_fusion.3
  264.5 2.9 multiply_bitcast_fusion.2
  267.4 10.8 %conditional.2 = (f32[128,4,2048]{2,1,0:T(4,128)}, f32[128,4]{1,0:T(8,128)S(1)}) conditional(s32[]{:T(128)} %convert_element_type.84, (f32[128,4,2048]{0,2,1:T(8,128)}) %tuple.68, (s32[]{:T(128)}, s32[]{:T(128)}, f32[128,4,2048]{0,2,1:T(8,128)}) %tuple.69), branch_computations={%region_9.0_spmd, %region_11.12_spmd} | conditional | flops 2104833 | bytes 16783400 | solution.py:41
  267.4 5.5 %copy.49 = f32[128,4,2048]{2,1,0:T(4,128)} copy(f32[128,4,2048]{0,2,1:T(8,128)} %get-tuple-element.233) | data formatting | bytes 8388608 | tf_op jit(solution)/shard_map
  272.9 5.3 %fusion.27 = (f32[128,4]{1,0:T(8,128)S(1)}, f32[128,4,2048]{2,1,0:T(4,128)}) fusion(f32[128,4,2048]{2,1,0:T(4,128)} %copy.49, pred[2048]{0:T(1024)(128)(4,1)S(1)} %fusion.2), kind=kLoop, calls=%fused_computation.39 | loop fusion | flops 2096640 | bytes 8392704 | tf_op jit(solution)/shard_map/while/body/eval_jaxpr/reduce_max | solution.py:42
  278.2 3.5 fusion.50
  281.8 3.7 fusion.51
  285.5 2.7 constant_dynamic-slice_fusion.3
  288.2 2.9 multiply_bitcast_fusion.2
  291.1 8.1 %conditional.2 = (f32[128,4,2048]{2,1,0:T(4,128)}, f32[128,4]{1,0:T(8,128)S(1)}) conditional(s32[]{:T(128)} %convert_element_type.84, (f32[128,4,2048]{0,2,1:T(8,128)}) %tuple.68, (s32[]{:T(128)}, s32[]{:T(128)}, f32[128,4,2048]{0,2,1:T(8,128)}) %tuple.69), branch_computations={%region_9.0_spmd, %region_11.12_spmd} | conditional | flops 2104833 | bytes 16783400 | solution.py:41
  291.1 2.5 reduce_max.27
  293.6 5.5 %copy.62 = f32[128,4,2048]{2,1,0:T(4,128)} copy(f32[128,4,2048]{0,2,1:T(8,128)} %get-tuple-element.243) | data formatting | bytes 8388608 | tf_op jit(solution)/shard_map/while/body/eval_jaxpr/mul | solution.py:31
  299.2 3.5 fusion.50
  302.8 3.7 fusion.51
  306.6 2.7 constant_dynamic-slice_fusion.3
  309.3 2.9 multiply_bitcast_fusion.2
  312.1 8.1 %conditional.2 = (f32[128,4,2048]{2,1,0:T(4,128)}, f32[128,4]{1,0:T(8,128)S(1)}) conditional(s32[]{:T(128)} %convert_element_type.84, (f32[128,4,2048]{0,2,1:T(8,128)}) %tuple.68, (s32[]{:T(128)}, s32[]{:T(128)}, f32[128,4,2048]{0,2,1:T(8,128)}) %tuple.69), branch_computations={%region_9.0_spmd, %region_11.12_spmd} | conditional | flops 2104833 | bytes 16783400 | solution.py:41
  312.1 2.5 reduce_max.27
  314.6 5.5 %copy.62 = f32[128,4,2048]{2,1,0:T(4,128)} copy(f32[128,4,2048]{0,2,1:T(8,128)} %get-tuple-element.243) | data formatting | bytes 8388608 | tf_op jit(solution)/shard_map/while/body/eval_jaxpr/mul | solution.py:31
  320.2 3.5 fusion.50
  323.9 3.7 fusion.51
  327.6 2.7 constant_dynamic-slice_fusion.3
  330.3 2.9 multiply_bitcast_fusion.2
  333.2 8.1 %conditional.2 = (f32[128,4,2048]{2,1,0:T(4,128)}, f32[128,4]{1,0:T(8,128)S(1)}) conditional(s32[]{:T(128)} %convert_element_type.84, (f32[128,4,2048]{0,2,1:T(8,128)}) %tuple.68, (s32[]{:T(128)}, s32[]{:T(128)}, f32[128,4,2048]{0,2,1:T(8,128)}) %tuple.69), branch_computations={%region_9.0_spmd, %region_11.12_spmd} | conditional | flops 2104833 | bytes 16783400 | solution.py:41
  333.2 2.5 reduce_max.27
  335.7 5.5 %copy.62 = f32[128,4,2048]{2,1,0:T(4,128)} copy(f32[128,4,2048]{0,2,1:T(8,128)} %get-tuple-element.243) | data formatting | bytes 8388608 | tf_op jit(solution)/shard_map/while/body/eval_jaxpr/mul | solution.py:31
  341.3 3.5 fusion.50
  344.9 3.7 fusion.51
  349.9 36.8 %reduce-scatter.2.cloned.1.call-done = bf16[128,320]{0,1:T(8,128)(2,1)} async-done(((bf16[128,1280]{0,1:T(8,128)(2,1)}), bf16[128,320]{0,1:T(8,128)(2,1)}) %reduce-scatter.2.cloned.1.call-update) | async-done | bytes 81936 | tf_op jit(solution)/shard_map/reduce_scatter | solution.py:103
  (66 shorter events, 12.7 us)
Async XLA Ops:
  6.5 342.2 %copy-start = (bf16[256,1280]{1,0:T(8,128)(2,1)S(1)}, bf16[256,1280]{1,0:T(8,128)(2,1)}, u32[]{:S(2)}) copy-start(bf16[256,1280]{1,0:T(8,128)(2,1)} %param.19) | copy-start | bytes 1966084
  6.5 254.0 %copy-start.1 = (bf16[128,1280]{1,0:T(8,128)(2,1)S(1)}, bf16[128,1280]{1,0:T(8,128)(2,1)}, u32[]{:S(2)}) copy-start(bf16[128,1280]{1,0:T(8,128)(2,1)} %param.13) | copy-start | bytes 983044
  6.5 254.0 %copy-start.3 = (f32[1280]{0:T(1024)S(1)}, f32[1280]{0:T(1024)}, u32[]{:S(2)}) copy-start(f32[1280]{0:T(1024)} %param.15) | copy-start | bytes 15364
  6.5 254.0 %copy-start.4 = (f32[1280]{0:T(1024)S(1)}, f32[1280]{0:T(1024)}, u32[]{:S(2)}) copy-start(f32[1280]{0:T(1024)} %param.14) | copy-start | bytes 15364
  6.5 254.0 %copy-start.2 = (bf16[1280,256]{1,0:T(8,128)(2,1)S(1)}, bf16[1280,256]{1,0:T(8,128)(2,1)}, u32[]{:S(2)}) copy-start(bf16[1280,256]{1,0:T(8,128)(2,1)} %param.17) | copy-start | bytes 1966084
  6.5 255.2 %all-gather.3.cloned.1.call-start = ((), (), s32[]{:S(2)}) async-start(), calls=%async_computation.1 | async-start | bytes 4259840 | tf_op jit(solution)/shard_map/all_gather | solution.py:94
  8.3 253.4 %all-gather.5.cloned.1.call-start = ((), (), s32[]{:S(2)}) async-start(), calls=%async_computation.2 | async-start | bytes 4259840 | tf_op jit(solution)/shard_map/all_gather | solution.py:95
  10.0 376.7 %reduce-scatter.2.cloned.1.call-start = ((), (), s32[]{:S(2)}) async-start(), calls=%async_computation.3 | async-start | bytes 409600 | tf_op jit(solution)/shard_map/reduce_scatter | solution.py:103
Sparse Core Ops, SparseCore 0:
  10.6 87.3 all-gather.2
  101.3 81.6 all-gather.4
  350.0 36.5 reduce-scatter.1
where the time goes:
time: 395 us; the launch traced here: 393 us
  blocking collectives  244 us (62%)
  local copies, waits for them, and re-layouts  37.8 us (10%)
  waiting for transfers between devices  36.8 us (9%)
  matrix products  31 us (8%)
  other arithmetic  29.4 us (7%)
  between operations  13.3 us (3%)
    psum x1, blocking collectives, per_device(): squares = lax.psum(jnp.sum(centered * centered, axis=(0, 2)), 'patch')  124 us
    psum x1, blocking collectives, per_device(): group_total = lax.psum(jnp.sum(grouped, axis=(0, 2)), 'patch')  120 us
    reduce_scatter x1, waiting for transfers between devices, per_device(): lax.psum_scatter(partial_out.astype(jnp.bfloat16), 'head', scatter_dimens...  36.8 us
    mul x3, local copies, waits for them, and re-layouts, one_block(): jnp.einsum('qhd,khd->qhk', queries, keys_block, preferred_element_type=jn...  16.5 us
    dot_general x4, matrix products, one_block(): jnp.einsum('qhk,khd->qhd', weights.astype(jnp.bfloat16), values_block, pr...  14.8 us
    convert_element_type x4, other arithmetic, one_block(): weights.astype(jnp.bfloat16)  14.1 us
    reduce_max x4, other arithmetic, one_block(): new_top = jnp.maximum(top, jnp.max(scores, axis=2))  12.7 us
    dot_general x4, matrix products, one_block(): jnp.einsum('qhd,khd->qhk', queries, keys_block, preferred_element_type=jn...  11.5 us
  transfers between devices with their start and end apart: 3, of which 1 were waited for; matrix products, arithmetic and copies ran while one was open for 2% of the time, Pallas kernels for 0%

commit v1 on v0

v1 whole, which is shorter than its diff:
```python
import functools

import jax
import jax.numpy as jnp
from jax import lax
from jax.experimental import pallas as pl
from jax.experimental.pallas import tpu as pltpu
from jax.sharding import PartitionSpec as P

HEAD_DIM = 64
GROUPS = 32
EPSILON = 1e-06
X = 4
CORES = 2
LANES = 128
MESH = pl.DeviceIdType.MESH
NT = (((1,), (1,)), ((), ()))
TN = (((0,), (0,)), ((), ()))
F32 = jnp.float32
BF16 = jnp.bfloat16


def three_parts(value):
    high = value.astype(BF16).astype(F32)
    rest = value - high
    middle = rest.astype(BF16).astype(F32)
    low = (rest - middle).astype(BF16).astype(F32)
    return [high, middle, low]


def stack_rows(rows, height):
    width = rows[0].shape[1]
    index = lax.broadcasted_iota(jnp.int32, (height, width), 0)
    stacked = jnp.zeros((height, width), F32)
    for i, row in enumerate(rows):
        stacked = jnp.where(index == i, row, stacked)
    return stacked.astype(BF16)


def kernel(
    n_patch,
    n_head,
    tokens,
    gain,
    bias,
    w_query,
    w_key,
    w_value,
    w_out,
    stale_keys,
    stale_values,
    out,
    tok_v,
    wq_v,
    wk_v,
    wv_v,
    wo_all,
    groups_v,
    kv,
    qbuf,
    osend,
    lsend,
    obuf,
    lbuf,
    att,
    st_send,
    st_a,
    st_b,
    ld_sem,
    wo_ld_sem,
    kv_ld_sem,
    sta_send,
    sta_recv,
    stb_send,
    stb_recv,
    kv_send,
    kv_recv,
    q_send,
    q_recv,
    o_send,
    o_recv,
    l_send,
    l_recv,
    wo_send,
    wo_recv,
    wf_send,
    wf_recv,
    att_send,
    att_recv,
):
    n_z = n_patch // (X * CORES)
    plane = X * CORES
    rows, channels = tok_v.shape
    per_group = channels // GROUPS
    own_stale = 2 * n_z
    me = lax.axis_index("patch")
    head = lax.axis_index("head")
    z = me // plane
    x = (me // CORES) % X
    core = me % CORES
    columns = channels // n_head
    wide = wo_all.shape[3]

    def at(zz, xx, cc):
        return {"patch": (zz * X + xx) * CORES + cc}

    def z_peer(k):
        return at((z + k) % n_z, x, core)

    def x_peer(k):
        return at(z, (x + k) % X, core)

    def plane_peer(k):
        rank = (x * CORES + core + k) % plane
        return {"patch": z * plane + rank}

    def head_peer(k):
        return {"head": (head + k) % n_head}

    sibling = at(z, x, 1 - core)

    def remote(src, dst, send, recv, device):
        return pltpu.make_async_remote_copy(
            src_ref=src, dst_ref=dst, send_sem=send, recv_sem=recv, device_id=device, device_id_type=MESH
        )

    barrier = pltpu.get_barrier_semaphore()
    peers = [plane_peer(k) for k in range(1, plane)]
    peers += [z_peer(k) for k in range(1, n_z)]
    peers += [head_peer(k) for k in range(1, n_head)]
    for peer in peers:
        pl.semaphore_signal(barrier, inc=1, device_id=peer, device_id_type=MESH)

    load_tok = pltpu.make_async_copy(tokens, tok_v, ld_sem.at[0])
    load_tok.start()
    load_kv = []
    for p in range(2):
        for which, source in enumerate((stale_keys, stale_values)):
            copy = pltpu.make_async_copy(
                source.at[:, p * LANES : (p + 1) * LANES], kv.at[p, own_stale, which], kv_ld_sem.at[p, which]
            )
            copy.start()
            load_kv.append(copy)
    load_w = [
        pltpu.make_async_copy(source, target, ld_sem.at[1 + i])
        for i, (source, target) in enumerate(((w_query, wq_v), (w_key, wk_v), (w_value, wv_v)))
    ]
    for copy in load_w:
        copy.start()

    def first_column(h):
        return pl.multiple_of((h * columns) // LANES * LANES, LANES)

    load_wo = [
        pltpu.make_async_copy(
            w_out.at[p * LANES : (p + 1) * LANES, pl.ds(first_column(head), wide)], wo_all.at[0, p], wo_ld_sem.at[p]
        )
        for p in range(2)
    ]
    for copy in load_wo:
        copy.start()

    channel = lax.broadcasted_iota(jnp.int32, (channels, LANES), 0)
    first = lax.broadcasted_iota(jnp.int32, (channels, LANES), 1) * per_group
    groups_v[...] = ((channel >= first) & (channel < first + per_group)).astype(F32).astype(BF16)

    def to_groups(row):
        parts = jnp.dot(stack_rows(three_parts(row), 16), groups_v[...], preferred_element_type=F32)
        return jnp.sum(parts, axis=0, keepdims=True)

    def to_channels(*values):
        stacked = stack_rows([part for value in values for part in three_parts(value)], 16)
        spread = lax.dot_general(stacked, groups_v[...], NT, preferred_element_type=F32)
        return [
            spread[3 * i : 3 * i + 1] + spread[3 * i + 1 : 3 * i + 2] + spread[3 * i + 2 : 3 * i + 3]
            for i in range(len(values))
        ]

    load_tok.wait()
    own_count = rows * per_group
    own_mean = to_groups(jnp.sum(tok_v[...].astype(F32), axis=0, keepdims=True)) * (1.0 / own_count)
    (shift,) = to_channels(own_mean)
    centred = tok_v[...].astype(F32) - shift
    own_squares = to_groups(jnp.sum(centred * centred, axis=0, keepdims=True))

    index8 = lax.broadcasted_iota(jnp.int32, (8, LANES), 0)

    def packet(mean, squares):
        return jnp.where(index8 == 0, mean, jnp.where(index8 == 1, squares, 0.0))

    def join(stats, count):
        shares = stats.shape[0]
        total = jnp.sum(stats, axis=0)
        mean = total * (1.0 / shares)
        apart = stats - mean[None]
        spread = jnp.sum(apart * apart, axis=0)
        return mean[0:1], total[1:2] + count * spread[0:1]

    own_packet = packet(own_mean, own_squares)
    st_send[0] = own_packet
    st_a[0] = own_packet

    pl.semaphore_wait(barrier, len(peers))

    stat_a = [
        remote(st_send.at[0], st_a.at[k], sta_send.at[k], sta_recv.at[k], plane_peer(k)) for k in range(1, plane)
    ]
    for copy in stat_a:
        copy.start()

    up = n_z // 2

    def kv_copy(p, src, dst, device):
        return remote(kv.at[p, src], kv.at[p, dst], kv_send.at[p, dst], kv_recv.at[p, dst], device)

    def kv_arrived(p, slot):
        kv_copy(p, own_stale, slot, sibling).wait_recv()

    def kv_first(p):
        load_kv[2 * p].wait()
        load_kv[2 * p + 1].wait()
        kv_copy(p, own_stale, 1, z_peer(1)).start()
        kv_copy(p, own_stale, up + 1, z_peer(n_z - 1)).start()
        kv_copy(p, own_stale, n_z, sibling).start()

    def kv_forward(p, step):
        kv_arrived(p, step)
        if step < up:
            kv_copy(p, step, step + 1, z_peer(1)).start()
        kv_copy(p, step, n_z + step, sibling).start()
        down = up + step
        if down < n_z:
            kv_arrived(p, down)
            if down + 1 < n_z:
                kv_copy(p, down, down + 1, z_peer(n_z - 1)).start()
            kv_copy(p, down, n_z + down, sibling).start()

    def kv_rest(p):
        for slot in range(n_z, 2 * n_z):
            kv_arrived(p, slot)

    kv_first(0)

    def wo_copy(k):
        return remote(
            w_out.at[pl.ds(core * LANES, LANES), pl.ds(first_column((head + k) % n_head), wide)],
            wo_all.at[n_head - k, core],
            wo_send.at[n_head - k],
            wo_recv.at[n_head - k],
            head_peer(k),
        )

    def wo_forward(s):
        return remote(wo_all.at[s, core], wo_all.at[s, core], wf_send.at[s], wf_recv.at[s], sibling)

    def wo_from_sibling(s):
        return remote(wo_all.at[s, core], wo_all.at[s, 1 - core], wf_send.at[s], wf_recv.at[s], sibling)

    for k in range(1, n_head):
        wo_copy(k).start()

    for copy in stat_a:
        copy.wait_recv()
    mean, squares = join(st_a[...], own_count)
    plane_packet = packet(mean, squares)
    st_send[1] = plane_packet
    st_b[0] = plane_packet
    stat_b = [remote(st_send.at[1], st_b.at[k], stb_send.at[k], stb_recv.at[k], z_peer(k)) for k in range(1, n_z)]
    for copy in stat_b:
        copy.start()

    kv_forward(0, 1)
    kv_first(1)

    for copy in stat_b:
        copy.wait_recv()
    mean, squares = join(st_b[...], own_count * plane)
    inverse = lax.rsqrt(squares * (1.0 / (own_count * n_patch)) + EPSILON)
    mean_of, inverse_of = to_channels(mean, inverse)
    normed = (tok_v[...].astype(F32) - mean_of) * inverse_of
    normed = (normed * gain[...].reshape(1, channels) + bias[...].reshape(1, channels)).astype(BF16)

    load_w[0].wait()
    query = jnp.dot(normed, wq_v[...], preferred_element_type=F32).astype(BF16) * jnp.asarray(0.125, BF16)
    q_copies = []
    for p in range(2):
        qbuf[0, p] = query[:, p * LANES : (p + 1) * LANES]

    def q_copy(p, k):
        return remote(
            qbuf.at[0, p], qbuf.at[X - k, p], q_send.at[X - k, p], q_recv.at[X - k, p], x_peer(k)
        )

    for p in range(2):
        for k in range(1, X):
            q_copy(p, k).start()

    kv_forward(0, 2)

    load_w[1].wait()
    fresh = jnp.dot(normed, wk_v[...], preferred_element_type=F32).astype(BF16)
    for p in range(2):
        kv[p, 0, 0] = fresh[:, p * LANES : (p + 1) * LANES]
    load_w[2].wait()
    fresh = jnp.dot(normed, wv_v[...], preferred_element_type=F32).astype(BF16)
    for p in range(2):
        kv[p, 0, 1] = fresh[:, p * LANES : (p + 1) * LANES]

    kv_forward(0, 3)
    kv_forward(1, 1)
    kv_forward(0, 4)
    kv_rest(0)

    lane = lax.broadcasted_iota(jnp.int32, (rows, LANES), 1)
    first_half = lane < HEAD_DIM
    blocks = 2
    ones = jnp.ones((blocks * rows, LANES), BF16)

    def o_copy(p, j):
        return remote(osend.at[p, j], obuf.at[p, X - j], o_send.at[p, j], o_recv.at[p, X - j], x_peer(j))

    def l_copy(p, j):
        return remote(lsend.at[p, j], lbuf.at[p, X - j], l_send.at[p, j], l_recv.at[p, X - j], x_peer(j))

    def attend(p, j):
        @pl.when(j != 0)
        def _():
            remote(qbuf.at[0, p], qbuf.at[j, p], q_send.at[j, p], q_recv.at[j, p], sibling).wait_recv()

        start = jnp.where(j == 0, 0, 1)
        q = qbuf[j, p]
        q_of = [jnp.where(first_half == (h == 0), q, jnp.zeros_like(q)) for h in range(2)]
        top, summed = [None, None], [None, None]
        for c in range(2 * n_z // blocks):
            keys = kv[p, pl.ds(start + blocks * c, blocks), 0].reshape(blocks * rows, LANES)
            values = kv[p, pl.ds(start + blocks * c, blocks), 1].reshape(blocks * rows, LANES)
            values = jnp.concatenate([values, ones], axis=1)
            for h in range(2):
                scores = lax.dot_general(q_of[h], keys, NT, preferred_element_type=F32)
                new_top = jnp.max(scores, axis=1, keepdims=True)
                if c:
                    new_top = jnp.maximum(top[h], new_top)
                weights = jnp.exp(scores - new_top).astype(BF16)
                more = jnp.dot(weights, values, preferred_element_type=F32)
                summed[h] = summed[h] * jnp.exp(top[h] - new_top) + more if c else more
                top[h] = new_top
        total = [summed[h][:, LANES:] for h in range(2)]
        osend[p, j] = jnp.where(
            first_half, summed[0][:, :LANES] / total[0], summed[1][:, :LANES] / total[1]
        ).astype(BF16)
        logs = jnp.where(lane == 0, top[0] + jnp.log(total[0]), top[1] + jnp.log(total[1]))
        lsend[p, j] = jnp.transpose(logs)[:8]

        @pl.when(j != 0)
        def _():
            o_copy(p, j).start()
            l_copy(p, j).start()

    def att_copy(p, k):
        return remote(
            att.at[0, p], att.at[n_head - k, p], att_send.at[n_head - k, p], att_recv.at[n_head - k, p], head_peer(k)
        )

    def combine(p):
        for s in range(1, X):
            o_copy(p, X - s).wait_recv()
            l_copy(p, X - s).wait_recv()
        logs = [lsend[p, 0]] + [lbuf[p, s] for s in range(1, X)]
        top = functools.reduce(jnp.maximum, logs)
        share = [jnp.exp(value - top) for value in logs]
        inverse_total = 1.0 / functools.reduce(jnp.add, share)
        parts = []
        for value in share:
            three = three_parts(value * inverse_total)
            parts.append(stack_rows([part[h : h + 1] for part in three for h in range(2)], 16))
        of_head = lax.broadcasted_iota(jnp.int32, (16, LANES), 0) % 2
        in_head = lax.broadcasted_iota(jnp.int32, (16, LANES), 1) // HEAD_DIM
        spread = (of_head == in_head).astype(F32).astype(BF16)
        joined = None
        for s in range(X):
            partial = osend[p, 0] if s == 0 else obuf[p, s]
            weight = lax.dot_general(parts[s], spread, TN, preferred_element_type=F32)
            term = weight * partial.astype(F32)
            joined = term if joined is None else joined + term
        att[0, p] = joined.astype(BF16)
        for k in range(1, n_head):
            att_copy(p, k).start()

    def first_pair(i, carry):
        attend(0, i)

        @pl.when(i == 0)
        def _():
            kv_forward(1, 2)

        @pl.when(i == 1)
        def _():
            kv_forward(1, 3)

        @pl.when(i == 2)
        def _():
            kv_forward(1, 4)

        return carry

    lax.fori_loop(0, X, first_pair, 0)
    kv_rest(1)
    for s in range(1, n_head):
        wo_copy(n_head - s).wait_recv()
        wo_forward(s).start()

    def second_pair(i, carry):
        attend(1, (i + 1) % X)

        @pl.when(i == 0)
        def _():
            combine(0)

        return carry

    lax.fori_loop(0, X, second_pair, 0)
    combine(1)

    for copy in load_wo:
        copy.wait()
    for s in range(1, n_head):
        wo_from_sibling(s).wait_recv()
    mixed = None
    for p in range(2):
        for s in range(n_head):
            if s:
                att_copy(p, n_head - s).wait_recv()
            term = jnp.dot(att[s, p], wo_all[s, p], preferred_element_type=F32)
            mixed = term if mixed is None else mixed + term
    shift = (head * columns) % LANES
    rolled = pltpu.roll(mixed, wide - LANES // 2, 1)
    mixed = jnp.where(shift == 0, mixed, rolled)
    out[...] = mixed[:, :columns].astype(BF16)

    for copy in stat_a + stat_b:
        copy.wait_send()
    for p in range(2):
        for slot in range(1, 2 * n_z):
            kv_copy(p, own_stale, slot, sibling).wait_send()
        for k in range(1, X):
            q_copy(p, k).wait_send()
            o_copy(p, k).wait_send()
            l_copy(p, k).wait_send()
        for k in range(1, n_head):
            att_copy(p, k).wait_send()
    for k in range(1, n_head):
        wo_copy(k).wait_send()
        wo_forward(k).wait_send()


def per_device(n_patch, n_head, *operands):
    tokens, _, _, w_query = operands[:4]
    rows, channels = tokens.shape
    inner = w_query.shape[1]
    n_z = n_patch // (X * CORES)
    columns = channels // n_head
    wide = -(-(columns + LANES // 2) // LANES) * LANES
    pairs = inner // LANES
    dma = pltpu.SemaphoreType.DMA
    any_space = pl.BlockSpec(memory_space=pl.ANY)
    vmem_space = pl.BlockSpec(memory_space=pltpu.VMEM)
    return pl.pallas_call(
        functools.partial(kernel, n_patch, n_head),
        out_shape=jax.ShapeDtypeStruct((rows, columns), BF16),
        in_specs=[any_space, vmem_space, vmem_space] + [any_space] * 6,
        out_specs=vmem_space,
        scratch_shapes=[
            pltpu.VMEM((rows, channels), BF16),
            pltpu.VMEM((channels, inner), BF16),
            pltpu.VMEM((channels, inner), BF16),
            pltpu.VMEM((channels, inner), BF16),
            pltpu.VMEM((n_head, pairs, LANES, wide), BF16),
            pltpu.VMEM((channels, LANES), BF16),
            pltpu.VMEM((pairs, 2 * n_z + 1, 2, rows, LANES), BF16),
            pltpu.VMEM((X, pairs, rows, LANES), BF16),
            pltpu.VMEM((pairs, X, rows, LANES), BF16),
            pltpu.VMEM((pairs, X, 8, LANES), F32),
            pltpu.VMEM((pairs, X, rows, LANES), BF16),
            pltpu.VMEM((pairs, X, 8, LANES), F32),
            pltpu.VMEM((n_head, pairs, rows, LANES), BF16),
            pltpu.VMEM((2, 8, LANES), F32),
            pltpu.VMEM((X * CORES, 8, LANES), F32),
            pltpu.VMEM((n_z, 8, LANES), F32),
            dma((4,)),
            dma((2,)),
            dma((2, 2)),
            dma((X * CORES,)),
            dma((X * CORES,)),
            dma((n_z,)),
            dma((n_z,)),
            dma((2, 2 * n_z)),
            dma((2, 2 * n_z)),
            dma((X, 2)),
            dma((X, 2)),
            dma((2, X)),
            dma((2, X)),
            dma((2, X)),
            dma((2, X)),
            dma((n_head,)),
            dma((n_head,)),
            dma((n_head,)),
            dma((n_head,)),
            dma((n_head, 2)),
            dma((n_head, 2)),
        ],
        compiler_params=pltpu.CompilerParams(
            collective_id=0, has_side_effects=True, vmem_limit_bytes=32 * 1024 * 1024
        ),
    )(*operands)


def solution(mesh):
    in_specs = (
        P(("cfg", "patch"), None),
        P(),
        P(),
        P(None, "head"),
        P(None, "head"),
        P(None, "head"),
        P("head", None),
        P(("cfg", "patch"), "head"),
        P(("cfg", "patch"), "head"),
    )
    return jax.shard_map(
        functools.partial(per_device, mesh.shape["patch"], mesh.shape["head"]),
        mesh=mesh,
        in_specs=in_specs,
        out_specs=P(("cfg", "patch"), "head"),
        check_vma=False,
    )
```

time: 395 us -> 65.9 us (0.17)
  blocking collectives: 244 us -> 0 us
  Pallas kernels: 0 us -> 55.5 us
  waiting for transfers between devices: 36.8 us -> 0 us
  matrix products: 31 us -> 0 us
  other arithmetic: 29.4 us -> 0 us
  local copies, waits for them, and re-layouts: 37.8 us -> 9.14 us
  between operations: 13.3 us -> 0.02 us
    psum x2 -> x0, blocking collectives: 244 us -> none  [the longest x1 124 us: per_device(): squares = lax.psum(jnp.sum(centered * centered, axis=(0, 2)), 'patch')]
    pallas_call x0 -> x1, Pallas kernels: none -> 55.5 us  [per_device(): pl.pallas_call(functools.partial(kernel, n_patch, n_head), out_shape=jax....]
    reduce_scatter x1 -> x0, waiting for transfers between devices: 36.8 us -> none  [per_device(): lax.psum_scatter(partial_out.astype(jnp.bfloat16), 'head', scatter_dimens...]
    dot_general x14 -> x0, matrix products: 31 us -> none  [the longest x4 14.8 us: one_block(): jnp.einsum('qhk,khd->qhd', weights.astype(jnp.bfloat16), values_block, pr...]
    mul x5 -> x0, local copies, waits for them, and re-layouts: 16.6 us -> none  [the longest x3 16.5 us: one_block(): jnp.einsum('qhd,khd->qhk', queries, keys_block, preferred_element_type=jn...]
    convert_element_type x5 -> x0, other arithmetic: 14.1 us -> none  [the longest x4 14.1 us: one_block(): weights.astype(jnp.bfloat16)]
    reduce_max x4 -> x0, other arithmetic: 12.7 us -> none  [one_block(): new_top = jnp.maximum(top, jnp.max(scores, axis=2))]
    dynamic_slice x4 -> x0, local copies, waits for them, and re-layouts: 10.8 us -> none  [one_block(): lax.dynamic_slice_in_dim(values_piece, offset, width, 0)]
  transfers between devices with their start and end apart: 3 -> 0, of which waited for: 1 -> 0; matrix products, arithmetic and copies ran while one was open for 2% -> 0% of each run, Pallas kernels for 0% -> 0%
where the time goes in v1:
time: 65.9 us; the launch traced here: 64.7 us
  Pallas kernels  55.5 us (84%)
  local copies, waits for them, and re-layouts  9.14 us (14%)
    pallas_call x1, Pallas kernels, per_device(): pl.pallas_call(functools.partial(kernel, n_patch, n_head), out_shape=jax....  55.5 us
    unnamed x18, local copies, waits for them, and re-layouts  8.39 us

profile of v1, /device:TPU:6, one launch (start us, length us, event | category | flops | bytes accessed | tf_op | source)
XLA Modules:
  0.0 64.7 jit_solution(7071587151071435449)
XLA Ops:
  0.0 0.0 copy-start
  0.0 1.1 %copy-done = bf16[1280,256]{1,0:T(8,128)(2,1)S(1)} copy-done((bf16[1280,256]{1,0:T(8,128)(2,1)S(1)}, bf16[1280,256]{1,0:T(8,128)(2,1)}, u32[]{:S(2)}) %copy-start) | copy-done | bytes 655384
  1.1 0.0 copy-start.1
  1.1 1.1 %copy-done.1 = bf16[1280,256]{1,0:T(8,128)(2,1)S(1)} copy-done((bf16[1280,256]{1,0:T(8,128)(2,1)S(1)}, bf16[1280,256]{1,0:T(8,128)(2,1)}, u32[]{:S(2)}) %copy-start.1) | copy-done | bytes 655384
  2.2 0.0 copy-start.2
  2.2 1.1 %copy-done.2 = bf16[1280,256]{1,0:T(8,128)(2,1)S(1)} copy-done((bf16[1280,256]{1,0:T(8,128)(2,1)S(1)}, bf16[1280,256]{1,0:T(8,128)(2,1)}, u32[]{:S(2)}) %copy-start.2) | copy-done | bytes 655384
  3.3 0.0 copy-start.3
  3.3 1.1 %copy-done.3 = bf16[256,1280]{1,0:T(8,128)(2,1)S(1)} copy-done((bf16[256,1280]{1,0:T(8,128)(2,1)S(1)}, bf16[256,1280]{1,0:T(8,128)(2,1)}, u32[]{:S(2)}) %copy-start.3) | copy-done | bytes 655384
  4.4 0.0 copy-start.4
  4.4 1.0 %copy-done.4 = bf16[128,1280]{1,0:T(8,128)(2,1)S(1)} copy-done((bf16[128,1280]{1,0:T(8,128)(2,1)S(1)}, bf16[128,1280]{1,0:T(8,128)(2,1)}, u32[]{:S(2)}) %copy-start.4) | copy-done | bytes 327704
  5.3 0.0 copy-start.5
  5.3 0.8 %copy-done.5 = bf16[128,256]{1,0:T(8,128)(2,1)S(1)} copy-done((bf16[128,256]{1,0:T(8,128)(2,1)S(1)}, bf16[128,256]{1,0:T(8,128)(2,1)}, u32[]{:S(2)}) %copy-start.5) | copy-done | bytes 65560
  6.2 0.0 copy-start.6
  6.2 0.8 %copy-done.6 = bf16[128,256]{1,0:T(8,128)(2,1)S(1)} copy-done((bf16[128,256]{1,0:T(8,128)(2,1)S(1)}, bf16[128,256]{1,0:T(8,128)(2,1)}, u32[]{:S(2)}) %copy-start.6) | copy-done | bytes 65560
  7.0 0.0 copy-start.7
  7.0 0.7 %copy-done.7 = f32[1280]{0:T(1024)S(1)} copy-done((f32[1280]{0:T(1024)S(1)}, f32[1280]{0:T(1024)}, u32[]{:S(2)}) %copy-start.7) | copy-done | bytes 5144
  7.7 0.0 copy-start.8
  7.7 0.7 %copy-done.8 = f32[1280]{0:T(1024)S(1)} copy-done((f32[1280]{0:T(1024)S(1)}, f32[1280]{0:T(1024)}, u32[]{:S(2)}) %copy-start.8) | copy-done | bytes 5144
  8.4 55.5 %shard_map.91 = bf16[128,320]{1,0:T(8,128)(2,1)S(1)} custom-call(bf16[128,1280]{1,0:T(8,128)(2,1)S(1)} %copy-done.4, f32[1280]{0:T(1024)S(1)} %copy-done.7, f32[1280]{0:T(1024)S(1)} %copy-done.8, bf16[1280,256]{1,0:T(8,128)(2,1)S(1)} %copy-done, bf16[1280,256]{1,0:T(8,128)(2,1)S(1)} %copy-done.1, bf16[1280,256]{1,0:T(8,128)(2,1)S(1)} %copy-done.2, ...), custom_call_target="tpu_custom_call" | custom-call | tf_op jit(solution)/shard_map/pallas_call | solution.py:467
  63.9 0.7 %copy.10 = bf16[128,320]{0,1:T(8,128)(2,1)} copy(bf16[128,320]{1,0:T(8,128)(2,1)S(1)} %shard_map.91) | data formatting | bytes 163840 | tf_op jit(solution)/shard_map/pallas_call | solution.py:467
Async XLA Ops:
  0.0 1.1 %copy-start = (bf16[1280,256]{1,0:T(8,128)(2,1)S(1)}, bf16[1280,256]{1,0:T(8,128)(2,1)}, u32[]{:S(2)}) copy-start(bf16[1280,256]{1,0:T(8,128)(2,1)} %w_query.1) | copy-start | bytes 1966084
  1.1 1.1 %copy-start.1 = (bf16[1280,256]{1,0:T(8,128)(2,1)S(1)}, bf16[1280,256]{1,0:T(8,128)(2,1)}, u32[]{:S(2)}) copy-start(bf16[1280,256]{1,0:T(8,128)(2,1)} %w_key.1) | copy-start | bytes 1966084
  2.2 1.1 %copy-start.2 = (bf16[1280,256]{1,0:T(8,128)(2,1)S(1)}, bf16[1280,256]{1,0:T(8,128)(2,1)}, u32[]{:S(2)}) copy-start(bf16[1280,256]{1,0:T(8,128)(2,1)} %w_value.1) | copy-start | bytes 1966084
  3.3 1.1 %copy-start.3 = (bf16[256,1280]{1,0:T(8,128)(2,1)S(1)}, bf16[256,1280]{1,0:T(8,128)(2,1)}, u32[]{:S(2)}) copy-start(bf16[256,1280]{1,0:T(8,128)(2,1)} %w_out.1) | copy-start | bytes 1966084
  4.4 1.0 %copy-start.4 = (bf16[128,1280]{1,0:T(8,128)(2,1)S(1)}, bf16[128,1280]{1,0:T(8,128)(2,1)}, u32[]{:S(2)}) copy-start(bf16[128,1280]{1,0:T(8,128)(2,1)} %tokens.1) | copy-start | bytes 983044
  5.3 0.8 %copy-start.5 = (bf16[128,256]{1,0:T(8,128)(2,1)S(1)}, bf16[128,256]{1,0:T(8,128)(2,1)}, u32[]{:S(2)}) copy-start(bf16[128,256]{1,0:T(8,128)(2,1)} %stale_keys.1) | copy-start | bytes 196612
  6.2 0.8 %copy-start.6 = (bf16[128,256]{1,0:T(8,128)(2,1)S(1)}, bf16[128,256]{1,0:T(8,128)(2,1)}, u32[]{:S(2)}) copy-start(bf16[128,256]{1,0:T(8,128)(2,1)} %stale_values.1) | copy-start | bytes 196612
  7.0 0.7 %copy-start.7 = (f32[1280]{0:T(1024)S(1)}, f32[1280]{0:T(1024)}, u32[]{:S(2)}) copy-start(f32[1280]{0:T(1024)} %gain.1) | copy-start | bytes 15364
  7.7 0.7 %copy-start.8 = (f32[1280]{0:T(1024)S(1)}, f32[1280]{0:T(1024)}, u32[]{:S(2)}) copy-start(f32[1280]{0:T(1024)} %bias.1) | copy-start | bytes 15364

commit v2 on v1

v2 whole, which is shorter than its diff:
```python
import functools

import jax
import jax.numpy as jnp
from jax import lax
from jax.experimental import pallas as pl
from jax.experimental.pallas import tpu as pltpu
from jax.sharding import PartitionSpec as P

HEAD_DIM = 64
GROUPS = 32
EPSILON = 1e-06
X = 4
CORES = 2
LANES = 128
MESH = pl.DeviceIdType.MESH
NT = (((1,), (1,)), ((), ()))
F32 = jnp.float32
BF16 = jnp.bfloat16


def three_parts(value):
    high = value.astype(BF16).astype(F32)
    rest = value - high
    middle = rest.astype(BF16).astype(F32)
    low = (rest - middle).astype(BF16).astype(F32)
    return [high, middle, low]


def stack_rows(rows, height):
    width = rows[0].shape[1]
    index = lax.broadcasted_iota(jnp.int32, (height, width), 0)
    stacked = jnp.zeros((height, width), F32)
    for i, row in enumerate(rows):
        stacked = jnp.where(index == i, row, stacked)
    return stacked.astype(BF16)


def kernel(
    n_patch,
    n_head,
    tokens,
    gain,
    bias,
    w_query,
    w_key,
    w_value,
    w_out,
    stale_keys,
    stale_values,
    out,
    gain_v,
    bias_v,
    tok_v,
    stv_v,
    wq_v,
    wk_v,
    wv_v,
    wo_all,
    wo_t,
    groups_v,
    kv,
    qbuf,
    osend,
    obuf,
    att,
    scores_a,
    scores_b,
    st_send,
    st_a,
    st_b,
    ld_sem,
    wo_ld_sem,
    sta_send,
    sta_recv,
    stb_send,
    stb_recv,
    kv_send,
    kv_recv,
    q_send,
    q_recv,
    o_send,
    o_recv,
    wo_send,
    wo_recv,
    wf_send,
    wf_recv,
    att_send,
    att_recv,
):
    n_z = n_patch // (X * CORES)
    plane = X * CORES
    rows, channels = tok_v.shape
    per_group = channels // GROUPS
    own_stale = 2 * n_z
    me = lax.axis_index("patch")
    head = lax.axis_index("head")
    z = me // plane
    x = (me // CORES) % X
    core = me % CORES
    columns = channels // n_head
    wide = wo_all.shape[3]

    def at(zz, xx, cc):
        return {"patch": (zz * X + xx) * CORES + cc}

    def z_peer(k):
        return at((z + k) % n_z, x, core)

    def x_peer(k):
        return at(z, (x + k) % X, core)

    def plane_peer(k):
        rank = (x * CORES + core + k) % plane
        return {"patch": z * plane + rank}

    def head_peer(k):
        return {"head": (head + k) % n_head}

    sibling = at(z, x, 1 - core)

    def remote(src, dst, send, recv, device):
        return pltpu.make_async_remote_copy(
            src_ref=src, dst_ref=dst, send_sem=send, recv_sem=recv, device_id=device, device_id_type=MESH
        )

    barrier = pltpu.get_barrier_semaphore()
    peers = [plane_peer(k) for k in range(1, plane)]
    peers += [z_peer(k) for k in range(1, n_z)]
    peers += [head_peer(k) for k in range(1, n_head)]
    for peer in peers:
        pl.semaphore_signal(barrier, inc=1, device_id=peer, device_id_type=MESH)

    def load(source, target, sem):
        copy = pltpu.make_async_copy(source, target, sem)
        copy.start()
        return copy

    load_tok = load(tokens, tok_v, ld_sem.at[0])
    load_stale = [
        load(stale_keys.at[:, p * LANES : (p + 1) * LANES], kv.at[p, own_stale, 0], ld_sem.at[1 + p]) for p in range(2)
    ]
    load_stale.append(load(stale_values, stv_v, ld_sem.at[3]))
    load_norm = [load(gain, gain_v, ld_sem.at[4]), load(bias, bias_v, ld_sem.at[5])]
    load_w = [
        load(source, target, ld_sem.at[6 + i])
        for i, (source, target) in enumerate(((w_query, wq_v), (w_key, wk_v), (w_value, wv_v)))
    ]

    def first_column(h):
        return pl.multiple_of((h * columns) // LANES * LANES, LANES)

    load_wo = [
        load(
            w_out.at[p * LANES : (p + 1) * LANES, pl.ds(first_column(head), wide)], wo_all.at[0, p], wo_ld_sem.at[p]
        )
        for p in range(2)
    ]

    channel = lax.broadcasted_iota(jnp.int32, (channels, LANES), 0)
    first = lax.broadcasted_iota(jnp.int32, (channels, LANES), 1) * per_group
    groups_v[...] = ((channel >= first) & (channel < first + per_group)).astype(F32).astype(BF16)

    def to_groups(row):
        parts = jnp.dot(stack_rows(three_parts(row), 16), groups_v[...], preferred_element_type=F32)
        return jnp.sum(parts, axis=0, keepdims=True)

    def to_channels(*values):
        stacked = stack_rows([part for value in values for part in three_parts(value)], 16)
        spread = lax.dot_general(stacked, groups_v[...], NT, preferred_element_type=F32)
        return [
            spread[3 * i : 3 * i + 1] + spread[3 * i + 1 : 3 * i + 2] + spread[3 * i + 2 : 3 * i + 3]
            for i in range(len(values))
        ]

    load_tok.wait()
    own_count = rows * per_group
    own_mean = to_groups(jnp.sum(tok_v[...].astype(F32), axis=0, keepdims=True)) * (1.0 / own_count)
    (shift,) = to_channels(own_mean)
    centred = tok_v[...].astype(F32) - shift
    own_squares = to_groups(jnp.sum(centred * centred, axis=0, keepdims=True))

    index8 = lax.broadcasted_iota(jnp.int32, (8, LANES), 0)

    def packet(mean, squares):
        return jnp.where(index8 == 0, mean, jnp.where(index8 == 1, squares, 0.0))

    def join(stats, count):
        shares = stats.shape[0]
        total = jnp.sum(stats, axis=0)
        mean = total * (1.0 / shares)
        apart = stats - mean[None]
        spread = jnp.sum(apart * apart, axis=0)
        return mean[0:1], total[1:2] + count * spread[0:1]

    own_packet = packet(own_mean, own_squares)
    st_send[0] = own_packet
    st_a[0] = own_packet
    for copy in load_stale:
        copy.wait()
    for p in range(2):
        kv[p, own_stale, 1] = jnp.transpose(stv_v[:, p * LANES : (p + 1) * LANES])

    pl.semaphore_wait(barrier, len(peers))

    stat_a = [
        remote(st_send.at[0], st_a.at[k], sta_send.at[k], sta_recv.at[k], plane_peer(k)) for k in range(1, plane)
    ]
    for copy in stat_a:
        copy.start()

    hops = n_z // 2

    def kv_copy(p, src, dst, device):
        return remote(kv.at[p, src], kv.at[p, dst], kv_send.at[p, dst], kv_recv.at[p, dst], device)

    def kv_arrived(p, slot):
        kv_copy(p, own_stale, slot, sibling).wait_recv()

    def kv_first(p):
        kv_copy(p, own_stale, 2, z_peer(1)).start()
        kv_copy(p, own_stale, 3, z_peer(n_z - 1)).start()
        kv_copy(p, own_stale, 1, sibling).start()

    def kv_forward(p, hop):
        slot = 4 * hop - 2
        kv_arrived(p, slot)
        if hop == hops:
            kv_copy(p, slot, slot + 1, sibling).start()
            return
        kv_copy(p, slot, slot + 4, z_peer(1)).start()
        kv_copy(p, slot, slot + 2, sibling).start()
        kv_arrived(p, slot + 1)
        if hop + 1 < hops:
            kv_copy(p, slot + 1, slot + 5, z_peer(n_z - 1)).start()
        kv_copy(p, slot + 1, slot + 3, sibling).start()

    for p in range(2):
        kv_first(p)

    def wo_copy(k):
        return remote(
            w_out.at[pl.ds(core * LANES, LANES), pl.ds(first_column((head + k) % n_head), wide)],
            wo_all.at[n_head - k, core],
            wo_send.at[n_head - k],
            wo_recv.at[n_head - k],
            head_peer(k),
        )

    def wo_forward(s):
        return remote(wo_all.at[s, core], wo_all.at[s, core], wf_send.at[s], wf_recv.at[s], sibling)

    def wo_from_sibling(s):
        return remote(wo_all.at[s, core], wo_all.at[s, 1 - core], wf_send.at[s], wf_recv.at[s], sibling)

    for k in range(1, n_head):
        wo_copy(k).start()

    for copy in stat_a:
        copy.wait_recv()
    mean, squares = join(st_a[...], own_count)
    plane_packet = packet(mean, squares)
    st_send[1] = plane_packet
    st_b[0] = plane_packet
    stat_b = [remote(st_send.at[1], st_b.at[k], stb_send.at[k], stb_recv.at[k], z_peer(k)) for k in range(1, n_z)]
    for copy in stat_b:
        copy.start()

    kv_forward(0, 1)
    kv_forward(1, 1)
    for copy in load_norm + load_w:
        copy.wait()
    kv_forward(0, 2)

    for copy in stat_b:
        copy.wait_recv()
    mean, squares = join(st_b[...], own_count * plane)
    inverse = lax.rsqrt(squares * (1.0 / (own_count * n_patch)) + EPSILON)
    mean_of, inverse_of = to_channels(mean, inverse)
    normed = (tok_v[...].astype(F32) - mean_of) * inverse_of
    normed = (normed * gain_v[...].reshape(1, channels) + bias_v[...].reshape(1, channels)).astype(BF16)

    query = jnp.dot(normed, wq_v[...], preferred_element_type=F32).astype(BF16) * jnp.asarray(0.125, BF16)
    for p in range(2):
        qbuf[0, p] = query[:, p * LANES : (p + 1) * LANES]

    def q_copy(p, k):
        return remote(qbuf.at[0, p], qbuf.at[X - k, p], q_send.at[X - k, p], q_recv.at[X - k, p], x_peer(k))

    for p in range(2):
        for k in range(1, X):
            q_copy(p, k).start()

    kv_forward(1, 2)

    fresh = jnp.dot(normed, wk_v[...], preferred_element_type=F32).astype(BF16)
    for p in range(2):
        kv[p, 0, 0] = fresh[:, p * LANES : (p + 1) * LANES]
    fresh = jnp.dot(normed, wv_v[...], preferred_element_type=F32)
    for p in range(2):
        kv[p, 0, 1] = jnp.transpose(fresh[:, p * LANES : (p + 1) * LANES]).astype(BF16)

    kv_forward(0, 3)
    kv_forward(1, 3)

    lane = lax.broadcasted_iota(jnp.int32, (rows, LANES), 1)
    blocks = 2
    span = blocks * rows
    chunks = 2 * n_z // blocks
    both = 2 * LANES

    def masked_queries(p, j):
        q = qbuf[j, p]
        return jnp.concatenate(
            [jnp.where((lane < HEAD_DIM) == (h == 0), q, jnp.zeros_like(q)) for h in range(2)], axis=0
        )

    def score_chunk(p, j, queries, c, scores_ref):
        start = (0 if j == 0 else 1) + blocks * c
        keys = kv[p, start : start + blocks, 0].reshape(span, LANES)
        scores = lax.dot_general(keys, queries, NT, preferred_element_type=F32)
        scores_ref[c * span : (c + 1) * span] = scores
        return jnp.max(scores.reshape(span // 8, 8, both), axis=0)

    def sum_chunk(p, j, top, c, scores_ref):
        start = (0 if j == 0 else 1) + blocks * c
        weights = jnp.exp(scores_ref[c * span : (c + 1) * span] - top)
        total = jnp.sum(weights.reshape(span // 8, 8, both), axis=0)
        values = jnp.concatenate([kv[p, start + i, 1] for i in range(blocks)], axis=1)
        return total, jnp.dot(values, weights.astype(BF16), preferred_element_type=F32)

    def o_copy(p, j):
        return remote(osend.at[p, j], obuf.at[p, X - j], o_send.at[p, j], o_recv.at[p, X - j], x_peer(j))

    def q_arrived(p, j):
        remote(qbuf.at[0, p], qbuf.at[j, p], q_send.at[j, p], q_recv.at[j, p], sibling).wait_recv()

    def finish(p, j, top, total, summed):
        total = jnp.sum(total, axis=0, keepdims=True)
        summed = summed * (1.0 / total)
        logs = top + jnp.log(total)
        osend[p, j, :rows] = jnp.concatenate(
            [summed[:HEAD_DIM, :LANES], summed[HEAD_DIM:, LANES:]], axis=0
        ).astype(BF16)
        three = three_parts(logs)
        osend[p, j, rows:] = stack_rows(
            [part[:, h * LANES : (h + 1) * LANES] for part in three for h in range(2)], 16
        )
        if j:
            o_copy(p, j).start()

    def att_copy(p, k):
        own = att.at[p, 0:rows]
        there = att.at[p, (n_head - k) * rows : (n_head - k + 1) * rows]
        return remote(own, there, att_send.at[n_head - k, p], att_recv.at[n_head - k, p], head_peer(k))

    def combine(p):
        for s in range(1, X):
            o_copy(p, X - s).wait_recv()
        partials = [osend[p, 0]] + [obuf[p, s] for s in range(1, X)]
        logs = []
        for partial in partials:
            parts = partial[rows:].astype(F32)
            logs.append([parts[h : h + 1] + parts[2 + h : 3 + h] + parts[4 + h : 5 + h] for h in range(2)])
        joined = []
        for h in range(2):
            top = functools.reduce(jnp.maximum, [value[h] for value in logs])
            share = [jnp.exp(value[h] - top) for value in logs]
            inverse_total = 1.0 / functools.reduce(jnp.add, share)
            terms = [
                partial[h * HEAD_DIM : (h + 1) * HEAD_DIM].astype(F32) * (value * inverse_total)
                for partial, value in zip(partials, share)
            ]
            joined.append(functools.reduce(jnp.add, terms))
        att[p, 0:rows] = jnp.concatenate(joined, axis=0).astype(BF16)
        for k in range(1, n_head):
            att_copy(p, k).start()

    units = [(0, 0)] + [(0, j) for j in range(1, X)] + [(1, j) for j in range(1, X)] + [(1, 0)]
    buffers = (scores_a, scores_b)

    queries = masked_queries(0, 0)
    top = None
    for c in range(chunks):
        if c == chunks - 1:
            kv_forward(0, hops)
            kv_forward(1, hops)
        for slot in range(blocks * c, blocks * (c + 1)):
            if slot and (slot == 1 or (slot - 2) % 4 >= 2 or slot == 2 * n_z - 1):
                kv_arrived(0, slot)
        more = score_chunk(0, 0, queries, c, scores_a)
        top = more if top is None else jnp.maximum(top, more)
    top = jnp.max(top, axis=0, keepdims=True)
    for i, (p, j) in enumerate(units):
        after = units[i + 1] if i + 1 < len(units) else None
        if after:
            if after[1]:
                q_arrived(*after)
            if after == (1, 1):
                for slot in range(1, 2 * n_z):
                    if slot == 1 or (slot - 2) % 4 >= 2 or slot == 2 * n_z - 1:
                        kv_arrived(1, slot)
            queries = masked_queries(*after)
        next_top, total, summed = None, None, None
        for c in range(chunks):
            if after:
                more = score_chunk(*after, queries, c, buffers[(i + 1) % 2])
                next_top = more if next_top is None else jnp.maximum(next_top, more)
            more, term = sum_chunk(p, j, top, c, buffers[i % 2])
            total = more if total is None else total + more
            summed = term if summed is None else summed + term
        finish(p, j, top, total, summed)
        if after:
            top = jnp.max(next_top, axis=0, keepdims=True)
        if i == 0:
            for s in range(1, n_head):
                wo_copy(n_head - s).wait_recv()
                wo_forward(s).start()
        if i == len(units) - 2:
            combine(0)

    for copy in load_wo:
        copy.wait()
    for s in range(1, n_head):
        wo_from_sibling(s).wait_recv()
    for p in range(2):
        for s in range(n_head):
            wo_t[p, :, s * LANES : (s + 1) * LANES] = jnp.transpose(wo_all[s, p])
    combine(1)

    mixed = None
    for p in range(2):
        for s in range(1, n_head):
            att_copy(p, n_head - s).wait_recv()
        term = jnp.dot(wo_t[p], att[p], preferred_element_type=F32)
        mixed = term if mixed is None else mixed + term
    shift = (head * columns) % LANES
    half = LANES // 2
    out[...] = jnp.where(shift == 0, mixed[:columns], mixed[half : half + columns]).astype(BF16)

    for copy in stat_a + stat_b:
        copy.wait_send()
    for p in range(2):
        for slot in range(1, 2 * n_z):
            kv_copy(p, own_stale, slot, sibling).wait_send()
        for k in range(1, X):
            q_copy(p, k).wait_send()
            o_copy(p, k).wait_send()
        for k in range(1, n_head):
            att_copy(p, k).wait_send()
    for k in range(1, n_head):
        wo_copy(k).wait_send()
        wo_forward(k).wait_send()


def per_device(n_patch, n_head, *operands):
    tokens, _, _, w_query = operands[:4]
    rows, channels = tokens.shape
    inner = w_query.shape[1]
    n_z = n_patch // (X * CORES)
    columns = channels // n_head
    wide = -(-(columns + LANES // 2) // LANES) * LANES
    pairs = inner // LANES
    dma = pltpu.SemaphoreType.DMA
    any_space = pl.BlockSpec(memory_space=pl.ANY)
    vmem_space = pl.BlockSpec(memory_space=pltpu.VMEM)
    mixed = pl.pallas_call(
        functools.partial(kernel, n_patch, n_head),
        out_shape=jax.ShapeDtypeStruct((columns, rows), BF16),
        in_specs=[any_space] * 9,
        out_specs=vmem_space,
        scratch_shapes=[
            pltpu.VMEM((channels,), F32),
            pltpu.VMEM((channels,), F32),
            pltpu.VMEM((rows, channels), BF16),
            pltpu.VMEM((rows, inner), BF16),
            pltpu.VMEM((channels, inner), BF16),
            pltpu.VMEM((channels, inner), BF16),
            pltpu.VMEM((channels, inner), BF16),
            pltpu.VMEM((n_head, pairs, LANES, wide), BF16),
            pltpu.VMEM((pairs, wide, n_head * LANES), BF16),
            pltpu.VMEM((channels, LANES), BF16),
            pltpu.VMEM((pairs, 2 * n_z + 1, 2, rows, LANES), BF16),
            pltpu.VMEM((X, pairs, rows, LANES), BF16),
            pltpu.VMEM((pairs, X, rows + 16, LANES), BF16),
            pltpu.VMEM((pairs, X, rows + 16, LANES), BF16),
            pltpu.VMEM((pairs, n_head * rows, LANES), BF16),
            pltpu.VMEM((2 * n_z * rows, 2 * LANES), F32),
            pltpu.VMEM((2 * n_z * rows, 2 * LANES), F32),
            pltpu.VMEM((2, 8, LANES), F32),
            pltpu.VMEM((X * CORES, 8, LANES), F32),
            pltpu.VMEM((n_z, 8, LANES), F32),
            dma((9,)),
            dma((2,)),
            dma((X * CORES,)),
            dma((X * CORES,)),
            dma((n_z,)),
            dma((n_z,)),
            dma((2, 2 * n_z)),
            dma((2, 2 * n_z)),
            dma((X, 2)),
            dma((X, 2)),
            dma((2, X)),
            dma((2, X)),
            dma((n_head,)),
            dma((n_head,)),
            dma((n_head,)),
            dma((n_head,)),
            dma((n_head, 2)),
            dma((n_head, 2)),
        ],
        compiler_params=pltpu.CompilerParams(
            collective_id=0, has_side_effects=True, vmem_limit_bytes=60 * 1024 * 1024
        ),
    )(*operands)
    return jnp.transpose(mixed)


def solution(mesh):
    in_specs = (
        P(("cfg", "patch"), None),
        P(),
        P(),
        P(None, "head"),
        P(None, "head"),
        P(None, "head"),
        P("head", None),
        P(("cfg", "patch"), "head"),
        P(("cfg", "patch"), "head"),
    )
    return jax.shard_map(
        functools.partial(per_device, mesh.shape["patch"], mesh.shape["head"]),
        mesh=mesh,
        in_specs=in_specs,
        out_specs=P(("cfg", "patch"), "head"),
        check_vma=False,
    )
```

time: 65.9 us -> 49.7 us (0.75)
  Pallas kernels: 55.5 us -> 47.4 us
  local copies, waits for them, and re-layouts: 9.14 us -> 1.53 us
    pallas_call x1, Pallas kernels: 55.5 us -> 47.4 us  [per_device(): pl.pallas_call(functools.partial(kernel, n_patch, n_head), out_shape=jax....]
    unnamed x18 -> x1, local copies, waits for them, and re-layouts: 8.39 us -> 1.53 us
    pallas_call x1 -> x0, local copies, waits for them, and re-layouts: 0.75 us -> none  [per_device(): pl.pallas_call(functools.partial(kernel, n_patch, n_head), out_shape=jax....]
where the time goes in v2:
time: 49.7 us; the launch traced here: 49 us
  Pallas kernels  47.4 us (95%)
  local copies, waits for them, and re-layouts  1.53 us (3%)
    pallas_call x1, Pallas kernels, per_device(): pl.pallas_call(functools.partial(kernel, n_patch, n_head), out_shape=jax....  47.4 us
    unnamed x1, local copies, waits for them, and re-layouts  1.53 us

profile of v2, /device:TPU:6, one launch (start us, length us, event | category | flops | bytes accessed | tf_op | source)
XLA Modules:
  0.0 49.0 jit_solution(3159880487353529890)
XLA Ops:
  0.0 47.4 %shard_map.91 = bf16[320,128]{1,0:T(8,128)(2,1)} custom-call(bf16[128,1280]{1,0:T(8,128)(2,1)} %tokens.1, f32[1280]{0:T(1024)} %gain.1, f32[1280]{0:T(1024)} %bias.1, bf16[1280,256]{1,0:T(8,128)(2,1)} %w_query.1, bf16[1280,256]{1,0:T(8,128)(2,1)} %w_key.1, bf16[1280,256]{1,0:T(8,128)(2,1)} %w_value.1, bf16[256,1280]{1,0:T(8,128)(2,1)} %w_out.1, ...), custom_call_target="tpu_custom_call" | custom-call | tf_op jit(solution)/shard_map/pallas_call | solution.py:467
  47.4 1.5 %copy.11 = bf16[128,320]{0,1:T(8,128)(2,1)} copy(bf16[128,320]{0,1:T(8,128)(2,1)} %bitcast.1) | data formatting | bytes 163840

commit v3 on v2

--- a/solution.py
+++ b/solution.py
@@ -75,8 +75,10 @@
     sta_recv,
     stb_send,
     stb_recv,
-    kv_send,
-    kv_recv,
+    kz_send,
+    kz_recv,
+    kc_send,
+    kc_recv,
     q_send,
     q_recv,
     o_send,
@@ -87,6 +89,8 @@
     wf_recv,
     att_send,
     att_recv,
+    near_sem,
+    far_head_sem,
 ):
     n_z = n_patch // (X * CORES)
     plane = X * CORES
@@ -126,8 +130,7 @@
 
     barrier = pltpu.get_barrier_semaphore()
     peers = [plane_peer(k) for k in range(1, plane)]
-    peers += [z_peer(k) for k in range(1, n_z)]
-    peers += [head_peer(k) for k in range(1, n_head)]
+    peers += [z_peer(1), z_peer(n_z - 1), head_peer(1), head_peer(n_head - 1)]
     for peer in peers:
         pl.semaphore_signal(barrier, inc=1, device_id=peer, device_id_type=MESH)
 
@@ -136,11 +139,11 @@
         copy.start()
         return copy
 
-    load_tok = load(tokens, tok_v, ld_sem.at[0])
     load_stale = [
         load(stale_keys.at[:, p * LANES : (p + 1) * LANES], kv.at[p, own_stale, 0], ld_sem.at[1 + p]) for p in range(2)
     ]
     load_stale.append(load(stale_values, stv_v, ld_sem.at[3]))
+    load_tok = load(tokens, tok_v, ld_sem.at[0])
     load_norm = [load(gain, gain_v, ld_sem.at[4]), load(bias, bias_v, ld_sem.at[5])]
     load_w = [
         load(source, target, ld_sem.at[6 + i])
@@ -156,6 +159,70 @@
         )
         for p in range(2)
     ]
+
+    hops = n_z // 2
+
+    def z_copy(p, which, src, dst, k):
+        return remote(
+            kv.at[p, src, which], kv.at[p, dst, which], kz_send.at[p, dst, which], kz_recv.at[p, dst, which], z_peer(k)
+        )
+
+    def core_copy(p, src, dst):
+        return remote(kv.at[p, src], kv.at[p, dst], kc_send.at[p, dst], kc_recv.at[p, dst], sibling)
+
+    def from_core(p, slot):
+        core_copy(p, own_stale, slot).wait_recv()
+
+    def kv_first(p, which):
+        z_copy(p, which, own_stale, 2, 1).start()
+        z_copy(p, which, own_stale, 3, n_z - 1).start()
+
+    def kv_forward(p, hop):
+        below, above = 4 * hop - 2, 4 * hop - 1
+        if hop == hops:
+            for which in range(2):
+                z_copy(p, which, own_stale, below, 1).wait_recv()
+            core_copy(p, below, below + 1).start()
+            return
+        for which in range(2):
+            z_copy(p, which, own_stale, below, 1).wait_recv()
+            if hop + 1 < hops or which == 0:
+                z_copy(p, which, below, below + 4, 1).start()
+            z_copy(p, which, own_stale, above, 1).wait_recv()
+            if hop + 1 < hops:
+                z_copy(p, which, above, above + 4, n_z - 1).start()
+            elif which == 1:
+                z_copy(p, which, above, below + 4, n_z - 1).start()
+        core_copy(p, below, below + 2).start()
+        core_copy(p, above, above + 2).start()
+
+    pl.semaphore_wait(barrier, len(peers))
+
+    def pass_on(rounds, up, down):
+        if up:
+            pl.semaphore_signal(near_sem.at[0, rounds], inc=1, device_id=z_peer(1), device_id_type=MESH)
+        if down:
+            pl.semaphore_signal(near_sem.at[1, rounds], inc=1, device_id=z_peer(n_z - 1), device_id_type=MESH)
+
+    def learn(rounds, up, down):
+        if up:
+            pl.semaphore_wait(near_sem.at[0, rounds], 1)
+        if down:
+            pl.semaphore_wait(near_sem.at[1, rounds], 1)
+
+    pass_on(0, True, True)
+    pl.semaphore_signal(far_head_sem, inc=1, device_id=head_peer(1), device_id_type=MESH)
+    load_stale[0].wait()
+    kv_first(0, 0)
+    load_stale[2].wait()
+    for p in range(2):
+        kv[p, own_stale, 1] = jnp.transpose(stv_v[:, p * LANES : (p + 1) * LANES])
+    kv_first(0, 1)
+    load_stale[1].wait()
+    kv_first(1, 0)
+    kv_first(1, 1)
+    for p in range(2):
+        core_copy(p, own_stale, 1).start()
 
     channel = lax.broadcasted_iota(jnp.int32, (channels, LANES), 0)
     first = lax.broadcasted_iota(jnp.int32, (channels, LANES), 1) * per_group
@@ -196,47 +263,13 @@
     own_packet = packet(own_mean, own_squares)
     st_send[0] = own_packet
     st_a[0] = own_packet
-    for copy in load_stale:
-        copy.wait()
-    for p in range(2):
-        kv[p, own_stale, 1] = jnp.transpose(stv_v[:, p * LANES : (p + 1) * LANES])
-
-    pl.semaphore_wait(barrier, len(peers))
-
+    learn(0, True, True)
+    pass_on(1, True, True)
     stat_a = [
         remote(st_send.at[0], st_a.at[k], sta_send.at[k], sta_recv.at[k], plane_peer(k)) for k in range(1, plane)
     ]
     for copy in stat_a:
         copy.start()
-
-    hops = n_z // 2
-
-    def kv_copy(p, src, dst, device):
-        return remote(kv.at[p, src], kv.at[p, dst], kv_send.at[p, dst], kv_recv.at[p, dst], device)
-
-    def kv_arrived(p, slot):
-        kv_copy(p, own_stale, slot, sibling).wait_recv()
-
-    def kv_first(p):
-        kv_copy(p, own_stale, 2, z_peer(1)).start()
-        kv_copy(p, own_stale, 3, z_peer(n_z - 1)).start()
-        kv_copy(p, own_stale, 1, sibling).start()
-
-    def kv_forward(p, hop):
-        slot = 4 * hop - 2
-        kv_arrived(p, slot)
-        if hop == hops:
-            kv_copy(p, slot, slot + 1, sibling).start()
-            return
-        kv_copy(p, slot, slot + 4, z_peer(1)).start()
-        kv_copy(p, slot, slot + 2, sibling).start()
-        kv_arrived(p, slot + 1)
-        if hop + 1 < hops:
-            kv_copy(p, slot + 1, slot + 5, z_peer(n_z - 1)).start()
-        kv_copy(p, slot + 1, slot + 3, sibling).start()
-
-    for p in range(2):
-        kv_first(p)
 
     def wo_copy(k):
         return remote(
@@ -253,24 +286,31 @@
     def wo_from_sibling(s):
         return remote(wo_all.at[s, core], wo_all.at[s, 1 - core], wf_send.at[s], wf_recv.at[s], sibling)
 
+    pl.semaphore_wait(far_head_sem, 1)
     for k in range(1, n_head):
         wo_copy(k).start()
 
+    kv_forward(0, 1)
+    learn(1, True, True)
+    pass_on(2, True, False)
+    kv_forward(1, 1)
     for copy in stat_a:
         copy.wait_recv()
     mean, squares = join(st_a[...], own_count)
     plane_packet = packet(mean, squares)
     st_send[1] = plane_packet
     st_b[0] = plane_packet
-    stat_b = [remote(st_send.at[1], st_b.at[k], stb_send.at[k], stb_recv.at[k], z_peer(k)) for k in range(1, n_z)]
+    far_first = sorted(range(1, n_z), key=lambda k: -min(k, n_z - k))
+    stat_b = [remote(st_send.at[1], st_b.at[k], stb_send.at[k], stb_recv.at[k], z_peer(k)) for k in far_first]
+    learn(2, True, False)
     for copy in stat_b:
         copy.start()
 
-    kv_forward(0, 1)
-    kv_forward(1, 1)
     for copy in load_norm + load_w:
         copy.wait()
     kv_forward(0, 2)
+    kv_forward(1, 2)
+    kv_forward(0, 3)
 
     for copy in stat_b:
         copy.wait_recv()
@@ -288,10 +328,10 @@
         return remote(qbuf.at[0, p], qbuf.at[X - k, p], q_send.at[X - k, p], q_recv.at[X - k, p], x_peer(k))
 
     for p in range(2):
-        for k in range(1, X):
+        for k in range(X - 1, 0, -1):
             q_copy(p, k).start()
 
-    kv_forward(1, 2)
+    kv_forward(1, 3)
 
     fresh = jnp.dot(normed, wk_v[...], preferred_element_type=F32).astype(BF16)
     for p in range(2):
@@ -299,9 +339,6 @@
     fresh = jnp.dot(normed, wv_v[...], preferred_element_type=F32)
     for p in range(2):
         kv[p, 0, 1] = jnp.transpose(fresh[:, p * LANES : (p + 1) * LANES]).astype(BF16)
-
-    kv_forward(0, 3)
-    kv_forward(1, 3)
 
     lane = lax.broadcasted_iota(jnp.int32, (rows, LANES), 1)
     blocks = 2
@@ -315,19 +352,28 @@
             [jnp.where((lane < HEAD_DIM) == (h == 0), q, jnp.zeros_like(q)) for h in range(2)], axis=0
         )
 
+    def slots_of(j, c):
+        return [slot if slot else (own_stale if j else 0) for slot in range(blocks * c, blocks * (c + 1))]
+
+    def scores_of(p, j, queries, c):
+        keys = jnp.concatenate([kv[p, slot, 0] for slot in slots_of(j, c)], axis=0)
+        return lax.dot_general(keys, queries, NT, preferred_element_type=F32)
+
+    def by_sublane(reduce, value):
+        return reduce(value.reshape(span // 8, 8, both), axis=0)
+
     def score_chunk(p, j, queries, c, scores_ref):
-        start = (0 if j == 0 else 1) + blocks * c
-        keys = kv[p, start : start + blocks, 0].reshape(span, LANES)
-        scores = lax.dot_general(keys, queries, NT, preferred_element_type=F32)
+        scores = scores_of(p, j, queries, c)
         scores_ref[c * span : (c + 1) * span] = scores
-        return jnp.max(scores.reshape(span // 8, 8, both), axis=0)
+        return by_sublane(jnp.max, scores)
+
+    def weigh(p, j, weights, c):
+        values = jnp.concatenate([kv[p, slot, 1] for slot in slots_of(j, c)], axis=1)
+        summed = jnp.dot(values, weights.astype(BF16), preferred_element_type=F32)
+        return by_sublane(jnp.sum, weights), summed
 
     def sum_chunk(p, j, top, c, scores_ref):
-        start = (0 if j == 0 else 1) + blocks * c
-        weights = jnp.exp(scores_ref[c * span : (c + 1) * span] - top)
-        total = jnp.sum(weights.reshape(span // 8, 8, both), axis=0)
-        values = jnp.concatenate([kv[p, start + i, 1] for i in range(blocks)], axis=1)
-        return total, jnp.dot(values, weights.astype(BF16), preferred_element_type=F32)
+        return weigh(p, j, jnp.exp(scores_ref[c * span : (c + 1) * span] - top), c)
 
     def o_copy(p, j):
         return remote(osend.at[p, j], obuf.at[p, X - j], o_send.at[p, j], o_recv.at[p, X - j], x_peer(j))
@@ -336,7 +382,6 @@
         remote(qbuf.at[0, p], qbuf.at[j, p], q_send.at[j, p], q_recv.at[j, p], sibling).wait_recv()
 
     def finish(p, j, top, total, summed):
-        total = jnp.sum(total, axis=0, keepdims=True)
         summed = summed * (1.0 / total)
         logs = top + jnp.log(total)
         osend[p, j, :rows] = jnp.concatenate(
@@ -373,51 +418,95 @@
             ]
             joined.append(functools.reduce(jnp.add, terms))
         att[p, 0:rows] = jnp.concatenate(joined, axis=0).astype(BF16)
-        for k in range(1, n_head):
+        for k in sorted(range(1, n_head), key=lambda k: -min(k, n_head - k)):
             att_copy(p, k).start()
 
-    units = [(0, 0)] + [(0, j) for j in range(1, X)] + [(1, j) for j in range(1, X)] + [(1, 0)]
+    core_slots = [slot for slot in range(1, 2 * n_z) if slot in (1, 2 * n_z - 1) or slot % 4 < 2]
+    last = chunks - 1
+
+    order = [(0, 0), (1, 0), (0, 1), (0, 2), (0, 3), (1, 2), (1, 1), (1, 3)]
+    early = 6
     buffers = (scores_a, scores_b)
 
-    queries = masked_queries(0, 0)
+    def arrive(i):
+        p, j = order[i]
+        if j:
+            q_arrived(p, j)
+        elif i:
+            for slot in core_slots[:-1]:
+                from_core(p, slot)
+
+    state = {}
+    tops, queries_of = {}, {}
+
+    def first_pass(i, c, top, buffer):
+        p, j = order[i]
+        more = score_chunk(p, j, queries_of[i], c, buffer)
+        return more if top is None else jnp.maximum(top, more)
+
+    def run(units):
+        for n, i in enumerate(units):
+            p, j = order[i]
+            after = units[n + 1] if n + 1 < len(units) else None
+            count = last if i < early else chunks
+            after_count = 0 if after is None else last if after < early else chunks
+            if after is not None:
+                arrive(after)
+                queries_of[after] = masked_queries(*order[after])
+            next_top, total, summed = None, None, None
+            for c in range(max(count, after_count)):
+                if c < after_count:
+                    next_top = first_pass(after, c, next_top, buffers[(n + 1) % 2])
+                if c < count:
+                    more, term = sum_chunk(p, j, tops[i], c, buffers[n % 2])
+                    total = more if total is None else total + more
+                    summed = term if summed is None else summed + term
+            total = jnp.sum(total, axis=0, keepdims=True)
+            if after is not None:
+                tops[after] = jnp.max(next_top, axis=0, keepdims=True)
+            if i < early:
+                state[i] = (tops[i], total, summed)
+            else:
+                finish(p, j, tops[i], total, summed)
+            if n == 1 and i < early:
+                kv_forward(0, hops)
+                kv_forward(1, hops)
+
+    def complete(units):
+        scores = [scores_of(*order[i], queries_of[i], last) for i in units]
+        for i, score in zip(units, scores):
+            p, j = order[i]
+            top, total, summed = state[i]
+            new_top = jnp.maximum(top, jnp.max(score, axis=0, keepdims=True))
+            factor = jnp.exp(top - new_top)
+            more, term = weigh(p, j, jnp.exp(score - new_top), last)
+            total = total * factor + jnp.sum(more, axis=0, keepdims=True)
+            finish(p, j, new_top, total, summed * factor + term)
+
+    queries_of[0] = masked_queries(*order[0])
+    top = None
+    for c in range(last):
+        for slot in range(blocks * c, blocks * (c + 1)):
+            if slot in core_slots:
+                from_core(0, slot)
+        top = first_pass(0, c, top, scores_a)
+    tops[0] = jnp.max(top, axis=0, keepdims=True)
+    run(list(range(early)))
+    for p in range(2):
+        from_core(p, 2 * n_z - 1)
+    complete([i for i in range(2, early)])
+    arrive(early)
+    queries_of[early] = masked_queries(*order[early])
     top = None
     for c in range(chunks):
-        if c == chunks - 1:
-            kv_forward(0, hops)
-            kv_forward(1, hops)
-        for slot in range(blocks * c, blocks * (c + 1)):
-            if slot and (slot == 1 or (slot - 2) % 4 >= 2 or slot == 2 * n_z - 1):
-                kv_arrived(0, slot)
-        more = score_chunk(0, 0, queries, c, scores_a)
-        top = more if top is None else jnp.maximum(top, more)
-    top = jnp.max(top, axis=0, keepdims=True)
-    for i, (p, j) in enumerate(units):
-        after = units[i + 1] if i + 1 < len(units) else None
-        if after:
-            if after[1]:
-                q_arrived(*after)
-            if after == (1, 1):
-                for slot in range(1, 2 * n_z):
-                    if slot == 1 or (slot - 2) % 4 >= 2 or slot == 2 * n_z - 1:
-                        kv_arrived(1, slot)
-            queries = masked_queries(*after)
-        next_top, total, summed = None, None, None
-        for c in range(chunks):
-            if after:
-                more = score_chunk(*after, queries, c, buffers[(i + 1) % 2])
-                next_top = more if next_top is None else jnp.maximum(next_top, more)
-            more, term = sum_chunk(p, j, top, c, buffers[i % 2])
-            total = more if total is None else total + more
-            summed = term if summed is None else summed + term
-        finish(p, j, top, total, summed)
-        if after:
-            top = jnp.max(next_top, axis=0, keepdims=True)
-        if i == 0:
-            for s in range(1, n_head):
-                wo_copy(n_head - s).wait_recv()
-                wo_forward(s).start()
-        if i == len(units) - 2:
-            combine(0)
+        top = first_pass(early, c, top, scores_a)
+    tops[early] = jnp.max(top, axis=0, keepdims=True)
+    run(list(range(early, len(order))))
+    for s in range(1, n_head):
+        wo_copy(n_head - s).wait_recv()
+        wo_forward(s).start()
+    complete([0, 1])
+    combine(0)
 
     for copy in load_wo:
         copy.wait()
@@ -426,6 +515,21 @@
     for p in range(2):
         for s in range(n_head):
             wo_t[p, :, s * LANES : (s + 1) * LANES] = jnp.transpose(wo_all[s, p])
+    for copy in stat_a + stat_b:
+        copy.wait_send()
+    for p in range(2):
+        for slot in range(2, 2 * n_z - 1):
+            if slot not in core_slots:
+                for which in range(2):
+                    z_copy(p, which, own_stale, slot, 1).wait_send()
+        for slot in core_slots:
+            core_copy(p, own_stale, slot).wait_send()
+        for k in range(1, X):
+            q_copy(p, k).wait_send()
+            o_copy(p, k).wait_send()
+    for k in range(1, n_head):
+        wo_copy(k).wait_send()
+        wo_forward(k).wait_send()
     combine(1)
 
     mixed = None
@@ -438,19 +542,9 @@
     half = LANES // 2
     out[...] = jnp.where(shift == 0, mixed[:columns], mixed[half : half + columns]).astype(BF16)
 
-    for copy in stat_a + stat_b:
-        copy.wait_send()
-    for p in range(2):
-        for slot in range(1, 2 * n_z):
-            kv_copy(p, own_stale, slot, sibling).wait_send()
-        for k in range(1, X):
-            q_copy(p, k).wait_send()
-            o_copy(p, k).wait_send()
+    for p in range(2):
         for k in range(1, n_head):
             att_copy(p, k).wait_send()
-    for k in range(1, n_head):
-        wo_copy(k).wait_send()
-        wo_forward(k).wait_send()
 
 
 def per_device(n_patch, n_head, *operands):
@@ -496,6 +590,8 @@
             dma((X * CORES,)),
             dma((n_z,)),
             dma((n_z,)),
+            dma((2, 2 * n_z, 2)),
+            dma((2, 2 * n_z, 2)),
             dma((2, 2 * n_z)),
             dma((2, 2 * n_z)),
             dma((X, 2)),
@@ -508,11 +604,13 @@
             dma((n_head,)),
             dma((n_head, 2)),
             dma((n_head, 2)),
+            pltpu.SemaphoreType.REGULAR((2, 3)),
+            pltpu.SemaphoreType.REGULAR,
         ],
         compiler_params=pltpu.CompilerParams(
-            collective_id=0, has_side_effects=True, vmem_limit_bytes=60 * 1024 * 1024
+            collective_id=0, has_side_effects=True, vmem_limit_bytes=40 * 1024 * 1024
         ),
-    )(*operands)
+    )(*[pltpu.with_memory_space_constraint(operand, pltpu.HBM) for operand in operands])
     return jnp.transpose(mixed)
 
 

time: 49.7 us -> 48.1 us (0.968); the launches traced: 49 us -> 48 us
  local copies, waits for them, and re-layouts: 1.53 us -> 0.64 us
    unnamed x1, local copies, waits for them, and re-layouts: 1.53 us -> 0.64 us
where the time goes in v3:
time: 48.1 us; the launch traced here: 48 us
  Pallas kernels  47.3 us (98%)
  local copies, waits for them, and re-layouts  0.64 us (1%)
    pallas_call x1, Pallas kernels, per_device(): pl.pallas_call(functools.partial(kernel, n_patch, n_head), out_shape=jax....  47.3 us

profile of v3, /device:TPU:6, one launch (start us, length us, event | category | flops | bytes accessed | tf_op | source)
XLA Modules:
  0.0 48.0 jit_solution(2305830255546337819)
XLA Ops:
  0.0 47.3 %shard_map.91 = bf16[320,128]{1,0:T(8,128)(2,1)S(1)} custom-call(bf16[128,1280]{1,0:T(8,128)(2,1)} %tokens.1, f32[1280]{0:T(1024)} %gain.1, f32[1280]{0:T(1024)} %bias.1, bf16[1280,256]{1,0:T(8,128)(2,1)} %w_query.1, bf16[1280,256]{1,0:T(8,128)(2,1)} %w_key.1, bf16[1280,256]{1,0:T(8,128)(2,1)} %w_value.1, bf16[256,1280]{1,0:T(8,128)(2,1)} %w_out.1, ...), custom_call_target="tpu_custom_call" | custom-call | tf_op jit(solution)/shard_map/pallas_call | solution.py:561
  47.3 0.6 %copy.11 = bf16[128,320]{0,1:T(8,128)(2,1)} copy(bf16[128,320]{0,1:T(8,128)(2,1)S(1)} %bitcast.1) | data formatting | bytes 163840

commit v4 on v3

v4 whole, which is shorter than its diff:
```python
import functools

import jax
import jax.numpy as jnp
from jax import lax
from jax.experimental import pallas as pl
from jax.experimental.pallas import tpu as pltpu
from jax.sharding import PartitionSpec as P

HEAD_DIM = 64
GROUPS = 32
EPSILON = 1e-06
X = 4
CORES = 2
LANES = 128
MESH = pl.DeviceIdType.MESH
NT = (((1,), (1,)), ((), ()))
F32 = jnp.float32
BF16 = jnp.bfloat16


def three_parts(value):
    high = value.astype(BF16).astype(F32)
    rest = value - high
    middle = rest.astype(BF16).astype(F32)
    low = (rest - middle).astype(BF16).astype(F32)
    return [high, middle, low]


def stack_rows(rows, height):
    width = rows[0].shape[1]
    index = lax.broadcasted_iota(jnp.int32, (height, width), 0)
    stacked = jnp.zeros((height, width), F32)
    for i, row in enumerate(rows):
        stacked = jnp.where(index == i, row, stacked)
    return stacked.astype(BF16)


def kernel(
    n_patch,
    n_head,
    tokens,
    gain,
    bias,
    w_query,
    w_key,
    w_value,
    w_out,
    stale_keys,
    stale_values,
    out,
    gain_v,
    bias_v,
    tok_v,
    stv_v,
    wq_v,
    wk_v,
    wv_v,
    wo_all,
    wo_t,
    groups_v,
    keys_v,
    values_v,
    qbuf,
    osend,
    obuf,
    att,
    scores_a,
    scores_b,
    st_send,
    st_a,
    st_b,
    ld_sem,
    wo_ld_sem,
    sib_send,
    sib_recv,
    sta_send,
    sta_recv,
    stb_send,
    stb_recv,
    kz_send,
    kz_recv,
    q_send,
    q_recv,
    o_send,
    o_recv,
    wo_send,
    wo_recv,
    wf_send,
    wf_recv,
    att_send,
    att_recv,
    near_sem,
    far_head_sem,
):
    n_z = n_patch // (X * CORES)
    plane = X * CORES
    rows, channels = tokens.shape
    chip_rows = CORES * rows
    per_group = channels // GROUPS
    fresh_slot = n_z
    me = lax.axis_index("patch")
    head = lax.axis_index("head")
    z = me // plane
    x = (me // CORES) % X
    core = me % CORES
    columns = channels // n_head
    wide = wo_all.shape[3]

    def at(zz, xx, cc):
        return {"patch": (zz * X + xx) * CORES + cc}

    def z_peer(k):
        return at((z + k) % n_z, x, core)

    def x_peer(k):
        return at(z, (x + k) % X, core)

    def plane_peer(k):
        rank = (x * CORES + core + k) % plane
        return {"patch": z * plane + rank}

    def head_peer(k):
        return {"head": (head + k) % n_head}

    sibling = at(z, x, 1 - core)

    def remote(src, dst, send, recv, device):
        return pltpu.make_async_remote_copy(
            src_ref=src, dst_ref=dst, send_sem=send, recv_sem=recv, device_id=device, device_id_type=MESH
        )

    barrier = pltpu.get_barrier_semaphore()
    peers = [plane_peer(k) for k in range(1, plane)]
    peers += [z_peer(1), z_peer(n_z - 1), head_peer(1), head_peer(n_head - 1)]
    for peer in peers:
        pl.semaphore_signal(barrier, inc=1, device_id=peer, device_id_type=MESH)

    def load(source, target, sem):
        copy = pltpu.make_async_copy(source, target, sem)
        copy.start()
        return copy

    own_pair = pl.ds(pl.multiple_of(core * LANES, LANES), LANES)
    other_pair = pl.ds(pl.multiple_of((1 - core) * LANES, LANES), LANES)
    load_tok = load(tokens, tok_v.at[0:rows], ld_sem.at[0])
    load_stale = [
        load(stale_keys.at[:, own_pair], keys_v.at[0, 0:rows], ld_sem.at[1]),
        load(stale_values.at[:, own_pair], stv_v.at[0:rows], ld_sem.at[2]),
    ]
    load_norm = [load(gain, gain_v, ld_sem.at[4]), load(bias, bias_v, ld_sem.at[5])]
    load_w = [
        load(source.at[:, own_pair], target, ld_sem.at[6 + i])
        for i, (source, target) in enumerate(((w_query, wq_v), (w_key, wk_v), (w_value, wv_v)))
    ]

    def first_column(h):
        return pl.multiple_of((h * columns) // LANES * LANES, LANES)

    load_wo = [
        load(
            w_out.at[pl.ds((core + r - 2 * core * r) * LANES, LANES), pl.ds(first_column(head), wide)],
            wo_all.at[0, r],
            wo_ld_sem.at[r],
        )
        for r in range(2)
    ]

    hops = n_z // 2
    held = (keys_v, values_v)

    def z_copy(which, src, dst, k):
        ref = held[which]
        return remote(ref.at[src], ref.at[dst], kz_send.at[dst, which], kz_recv.at[dst, which], z_peer(k))

    def kv_first(which):
        z_copy(which, 0, 1, 1).start()
        z_copy(which, 0, 2, n_z - 1).start()

    def kv_arrived(which, slot):
        z_copy(which, 0, slot, 1).wait_recv()

    def kv_forward(hop):
        below, above = 2 * hop - 1, 2 * hop
        for which in range(2):
            kv_arrived(which, below)
            if hop + 1 < hops or which == 0:
                z_copy(which, below, below + 2, 1).start()
            kv_arrived(which, above)
            if hop + 1 < hops:
                z_copy(which, above, above + 2, n_z - 1).start()
            elif which == 1:
                z_copy(which, above, below + 2, n_z - 1).start()

    channel = lax.broadcasted_iota(jnp.int32, (channels, LANES), 0)
    first = lax.broadcasted_iota(jnp.int32, (channels, LANES), 1) * per_group
    groups_v[...] = ((channel >= first) & (channel < first + per_group)).astype(F32).astype(BF16)

    def to_groups(row):
        parts = jnp.dot(stack_rows(three_parts(row), 16), groups_v[...], preferred_element_type=F32)
        return jnp.sum(parts, axis=0, keepdims=True)

    def to_channels(*values):
        stacked = stack_rows([part for value in values for part in three_parts(value)], 16)
        spread = lax.dot_general(stacked, groups_v[...], NT, preferred_element_type=F32)
        return [
            spread[3 * i : 3 * i + 1] + spread[3 * i + 1 : 3 * i + 2] + spread[3 * i + 2 : 3 * i + 3]
            for i in range(len(values))
        ]

    load_tok.wait()
    own_count = rows * per_group
    own_mean = to_groups(jnp.sum(tok_v[0:rows].astype(F32), axis=0, keepdims=True)) * (1.0 / own_count)
    (shift,) = to_channels(own_mean)
    centred = tok_v[0:rows].astype(F32) - shift
    own_squares = to_groups(jnp.sum(centred * centred, axis=0, keepdims=True))

    index8 = lax.broadcasted_iota(jnp.int32, (8, LANES), 0)

    def packet(mean, squares):
        return jnp.where(index8 == 0, mean, jnp.where(index8 == 1, squares, 0.0))

    def join(stats, count):
        shares = stats.shape[0]
        total = jnp.sum(stats, axis=0)
        mean = total * (1.0 / shares)
        apart = stats - mean[None]
        spread = jnp.sum(apart * apart, axis=0)
        return mean[0:1], total[1:2] + count * spread[0:1]

    own_packet = packet(own_mean, own_squares)
    st_send[0] = own_packet
    st_a[0] = own_packet
    pl.semaphore_wait(barrier, len(peers))

    def pass_on(rounds, up, down):
        if up:
            pl.semaphore_signal(near_sem.at[0, rounds], inc=1, device_id=z_peer(1), device_id_type=MESH)
        if down:
            pl.semaphore_signal(near_sem.at[1, rounds], inc=1, device_id=z_peer(n_z - 1), device_id_type=MESH)

    def learn(rounds, up, down):
        if up:
            pl.semaphore_wait(near_sem.at[0, rounds], 1)
        if down:
            pl.semaphore_wait(near_sem.at[1, rounds], 1)

    pass_on(0, True, True)
    pl.semaphore_signal(far_head_sem, inc=1, device_id=head_peer(1), device_id_type=MESH)
    to_sibling = [
        remote(stale_keys.at[:, other_pair], keys_v.at[0, rows:chip_rows], sib_send.at[0], sib_recv.at[0], sibling),
        remote(stale_values.at[:, other_pair], stv_v.at[rows:chip_rows], sib_send.at[1], sib_recv.at[1], sibling),
        remote(tokens, tok_v.at[rows:chip_rows], sib_send.at[2], sib_recv.at[2], sibling),
    ]
    for copy in to_sibling:
        copy.start()
    learn(0, True, True)
    pass_on(1, True, True)
    stat_a = [
        remote(st_send.at[0], st_a.at[k], sta_send.at[k], sta_recv.at[k], plane_peer(k)) for k in range(1, plane)
    ]
    for copy in stat_a:
        copy.start()
    load_stale[0].wait()
    to_sibling[0].wait_recv()
    kv_first(0)
    load_stale[1].wait()
    to_sibling[1].wait_recv()
    values_v[0] = jnp.transpose(stv_v[...])
    kv_first(1)


    def wo_copy(k):
        return remote(
            w_out.at[pl.ds(core * LANES, LANES), pl.ds(first_column((head + k) % n_head), wide)],
            wo_all.at[n_head - k, 0],
            wo_send.at[n_head - k],
            wo_recv.at[n_head - k],
            head_peer(k),
        )

    def wo_forward(s):
        return remote(wo_all.at[s, 0], wo_all.at[s, 1], wf_send.at[s], wf_recv.at[s], sibling)

    pl.semaphore_wait(far_head_sem, 1)
    for k in range(1, n_head):
        wo_copy(k).start()

    learn(1, True, True)
    pass_on(2, True, False)
    for copy in stat_a:
        copy.wait_recv()
    mean, squares = join(st_a[...], own_count)
    plane_packet = packet(mean, squares)
    st_send[1] = plane_packet
    st_b[0] = plane_packet
    far_first = sorted(range(1, n_z), key=lambda k: -min(k, n_z - k))
    stat_b = [remote(st_send.at[1], st_b.at[k], stb_send.at[k], stb_recv.at[k], z_peer(k)) for k in far_first]
    learn(2, True, False)
    for copy in stat_b:
        copy.start()

    for copy in load_norm + load_w:
        copy.wait()
    kv_forward(1)
    kv_forward(2)
    to_sibling[2].wait_recv()

    for copy in stat_b:
        copy.wait_recv()
    mean, squares = join(st_b[...], own_count * plane)
    inverse = lax.rsqrt(squares * (1.0 / (own_count * n_patch)) + EPSILON)
    mean_of, inverse_of = to_channels(mean, inverse)
    normed = (tok_v[...].astype(F32) - mean_of) * inverse_of
    normed = (normed * gain_v[...].reshape(1, channels) + bias_v[...].reshape(1, channels)).astype(BF16)

    query = jnp.dot(normed, wq_v[...], preferred_element_type=F32).astype(BF16) * jnp.asarray(0.125, BF16)
    qbuf[0] = query

    def q_copy(k, t):
        part = slice(t * rows, (t + 1) * rows)
        there = X - k
        return remote(qbuf.at[0, part], qbuf.at[there, part], q_send.at[there, t], q_recv.at[there, t], x_peer(k))

    for t in range(CORES):
        for k in range(X - 1, 0, -1):
            q_copy(k, t).start()

    keys_v[fresh_slot] = jnp.dot(normed, wk_v[...], preferred_element_type=F32).astype(BF16)
    fresh = jnp.dot(normed, wv_v[...], preferred_element_type=F32)
    values_v[fresh_slot] = jnp.transpose(fresh).astype(BF16)
    kv_forward(3)
    lane = lax.broadcasted_iota(jnp.int32, (rows, LANES), 1)
    span = chip_rows
    chunks = n_z
    both = 2 * LANES

    def masked_queries(j, t):
        q = qbuf[j, t * rows : (t + 1) * rows]
        return jnp.concatenate(
            [jnp.where((lane < HEAD_DIM) == (h == 0), q, jnp.zeros_like(q)) for h in range(2)], axis=0
        )

    def slot_of(j, t, c, half):
        return fresh_slot if (j, c, half) == (0, 0, t) else c

    def keys_of(j, t, c):
        return jnp.concatenate(
            [keys_v[slot_of(j, t, c, half), half * rows : (half + 1) * rows] for half in range(CORES)], axis=0
        )

    def values_of(j, t, c):
        return jnp.concatenate(
            [values_v[slot_of(j, t, c, half), :, half * rows : (half + 1) * rows] for half in range(CORES)], axis=1
        )

    def scores_of(j, t, queries, c):
        return lax.dot_general(keys_of(j, t, c), queries, NT, preferred_element_type=F32)

    def by_sublane(reduce, value):
        return reduce(value.reshape(span // 8, 8, both), axis=0)

    def score_chunk(j, t, queries, c, scores_ref):
        scores = scores_of(j, t, queries, c)
        scores_ref[c * span : (c + 1) * span] = scores
        return by_sublane(jnp.max, scores)

    def weigh(j, t, weights, c):
        summed = jnp.dot(values_of(j, t, c), weights.astype(BF16), preferred_element_type=F32)
        return by_sublane(jnp.sum, weights), summed

    def sum_chunk(j, t, top, c, scores_ref):
        return weigh(j, t, jnp.exp(scores_ref[c * span : (c + 1) * span] - top), c)

    def o_copy(j, t):
        owner = at(z, (x + j) % X, core + t - 2 * core * t)
        there = (X - j) % X
        return remote(osend.at[j, t], obuf.at[t, there], o_send.at[j, t], o_recv.at[t, there], owner)

    def q_arrived(j, t):
        q_copy(X - j, t).wait_recv()

    def finish(j, t, top, total, summed):
        summed = summed * (1.0 / total)
        logs = top + jnp.log(total)
        osend[j, t, :rows] = jnp.concatenate(
            [summed[:HEAD_DIM, :LANES], summed[HEAD_DIM:, LANES:]], axis=0
        ).astype(BF16)
        three = three_parts(logs)
        osend[j, t, rows:] = stack_rows(
            [part[:, h * LANES : (h + 1) * LANES] for part in three for h in range(2)], 16
        )
        if j or t:
            o_copy(j, t).start()

    def att_copy(p, k):
        own = att.at[p, 0:rows]
        there = att.at[p, (n_head - k) * rows : (n_head - k + 1) * rows]
        return remote(own, there, att_send.at[n_head - k, p], att_recv.at[n_head - k, p], head_peer(k))

    def combine(p):
        for s in range(X):
            if s or p:
                o_copy((X - s) % X, p).wait_recv()
        partials = [obuf[p, s] if s or p else osend[0, 0] for s in range(X)]
        logs = []
        for partial in partials:
            parts = partial[rows:].astype(F32)
            logs.append([parts[h : h + 1] + parts[2 + h : 3 + h] + parts[4 + h : 5 + h] for h in range(2)])
        joined = []
        for h in range(2):
            top = functools.reduce(jnp.maximum, [value[h] for value in logs])
            share = [jnp.exp(value[h] - top) for value in logs]
            inverse_total = 1.0 / functools.reduce(jnp.add, share)
            terms = [
                partial[h * HEAD_DIM : (h + 1) * HEAD_DIM].astype(F32) * (value * inverse_total)
                for partial, value in zip(partials, share)
            ]
            joined.append(functools.reduce(jnp.add, terms))
        att[p, 0:rows] = jnp.concatenate(joined, axis=0).astype(BF16)
        for k in sorted(range(1, n_head), key=lambda k: -min(k, n_head - k)):
            att_copy(p, k).start()

    order = [(0, 0), (0, 1), (1, 0), (3, 0), (2, 0), (2, 1), (1, 1), (3, 1)]
    early = 5
    last = chunks - 1
    buffers = (scores_a, scores_b)
    state, tops, queries_of = {}, {}, {}

    def arrive(i):
        j, t = order[i]
        if j:
            q_arrived(j, t)
        queries_of[i] = masked_queries(j, t)

    def first_pass(i, c, top, buffer):
        more = score_chunk(*order[i], queries_of[i], c, buffer)
        return more if top is None else jnp.maximum(top, more)

    def count_of(i):
        return last if i < early else chunks

    def run(units):
        arrive(units[0])
        top = None
        for c in range(count_of(units[0])):
            top = first_pass(units[0], c, top, scores_a)
        tops[units[0]] = jnp.max(top, axis=0, keepdims=True)
        for n, i in enumerate(units):
            j, t = order[i]
            after = units[n + 1] if n + 1 < len(units) else None
            after_count = 0 if after is None else count_of(after)
            if after is not None:
                arrive(after)
            next_top, total, summed = None, None, None
            for c in range(max(count_of(i), after_count)):
                if c < after_count:
                    next_top = first_pass(after, c, next_top, buffers[(n + 1) % 2])
                if c < count_of(i):
                    more, term = sum_chunk(j, t, tops[i], c, buffers[n % 2])
                    total = more if total is None else total + more
                    summed = term if summed is None else summed + term
            total = jnp.sum(total, axis=0, keepdims=True)
            if after is not None:
                tops[after] = jnp.max(next_top, axis=0, keepdims=True)
            if i < early:
                state[i] = (tops[i], total, summed)
            else:
                finish(j, t, tops[i], total, summed)

    def complete(units):
        scores = [scores_of(*order[i], queries_of[i], last) for i in units]
        for i, score in zip(units, scores):
            j, t = order[i]
            top, total, summed = state[i]
            new_top = jnp.maximum(top, jnp.max(score, axis=0, keepdims=True))
            factor = jnp.exp(top - new_top)
            more, term = weigh(j, t, jnp.exp(score - new_top), last)
            total = total * factor + jnp.sum(more, axis=0, keepdims=True)
            finish(j, t, new_top, total, summed * factor + term)

    run(list(range(early)))
    for s in range(1, n_head):
        wo_copy(n_head - s).wait_recv()
        wo_forward(s).start()
    for which in range(2):
        kv_arrived(which, last)
    complete([i for i in range(2, early) if not order[i][1]])
    if early > X + 1:
        complete(list(range(X + 1, early)))
    if early < len(order):
        run(list(range(early, len(order))))
    complete([1, 0])
    combine(0)

    combine(1)

    for copy in load_wo:
        copy.wait()
    for s in range(1, n_head):
        wo_forward(s).wait_recv()
    for p in range(2):
        for s in range(n_head):
            wo_t[p, :, s * LANES : (s + 1) * LANES] = jnp.transpose(wo_all[s, p])
    for copy in stat_a + stat_b:
        copy.wait_send()
    for copy in to_sibling:
        copy.wait_send()
    for slot in range(1, n_z):
        for which in range(2):
            z_copy(which, 0, slot, 1).wait_send()
    for k in range(1, X):
        for t in range(CORES):
            q_copy(k, t).wait_send()
    for j, t in order[1:]:
        o_copy(j, t).wait_send()
    for k in range(1, n_head):
        wo_copy(k).wait_send()
        wo_forward(k).wait_send()

    mixed = None
    for p in range(2):
        for s in range(1, n_head):
            att_copy(p, n_head - s).wait_recv()
        term = jnp.dot(wo_t[p], att[p], preferred_element_type=F32)
        mixed = term if mixed is None else mixed + term
    shift = (head * columns) % LANES
    half = LANES // 2
    out[...] = jnp.where(shift == 0, mixed[:columns], mixed[half : half + columns]).astype(BF16)

    for p in range(2):
        for k in range(1, n_head):
            att_copy(p, k).wait_send()


def per_device(n_patch, n_head, *operands):
    tokens, _, _, w_query = operands[:4]
    rows, channels = tokens.shape
    inner = w_query.shape[1]
    n_z = n_patch // (X * CORES)
    columns = channels // n_head
    wide = -(-(columns + LANES // 2) // LANES) * LANES
    pairs = inner // LANES
    dma = pltpu.SemaphoreType.DMA
    any_space = pl.BlockSpec(memory_space=pl.ANY)
    vmem_space = pl.BlockSpec(memory_space=pltpu.VMEM)
    mixed = pl.pallas_call(
        functools.partial(kernel, n_patch, n_head),
        out_shape=jax.ShapeDtypeStruct((columns, rows), BF16),
        in_specs=[any_space] * 9,
        out_specs=vmem_space,
        scratch_shapes=[
            pltpu.VMEM((channels,), F32),
            pltpu.VMEM((channels,), F32),
            pltpu.VMEM((CORES * rows, channels), BF16),
            pltpu.VMEM((CORES * rows, LANES), BF16),
            pltpu.VMEM((channels, LANES), BF16),
            pltpu.VMEM((channels, LANES), BF16),
            pltpu.VMEM((channels, LANES), BF16),
            pltpu.VMEM((n_head, pairs, LANES, wide), BF16),
            pltpu.VMEM((pairs, wide, n_head * LANES), BF16),
            pltpu.VMEM((channels, LANES), BF16),
            pltpu.VMEM((n_z + 1, CORES * rows, LANES), BF16),
            pltpu.VMEM((n_z + 1, LANES, CORES * rows), BF16),
            pltpu.VMEM((X, CORES * rows, LANES), BF16),
            pltpu.VMEM((X, CORES, rows + 16, LANES), BF16),
            pltpu.VMEM((pairs, X, rows + 16, LANES), BF16),
            pltpu.VMEM((pairs, n_head * rows, LANES), BF16),
            pltpu.VMEM((n_z * CORES * rows, 2 * LANES), F32),
            pltpu.VMEM((n_z * CORES * rows, 2 * LANES), F32),
            pltpu.VMEM((2, 8, LANES), F32),
            pltpu.VMEM((X * CORES, 8, LANES), F32),
            pltpu.VMEM((n_z, 8, LANES), F32),
            dma((9,)),
            dma((2,)),
            dma((3,)),
            dma((3,)),
            dma((X * CORES,)),
            dma((X * CORES,)),
            dma((n_z,)),
            dma((n_z,)),
            dma((n_z, 2)),
            dma((n_z, 2)),
            dma((X, CORES)),
            dma((X, CORES)),
            dma((X, CORES)),
            dma((pairs, X)),
            dma((n_head,)),
            dma((n_head,)),
            dma((n_head,)),
            dma((n_head,)),
            dma((n_head, 2)),
            dma((n_head, 2)),
            pltpu.SemaphoreType.REGULAR((2, 3)),
            pltpu.SemaphoreType.REGULAR,
        ],
        compiler_params=pltpu.CompilerParams(
            collective_id=0, has_side_effects=True, vmem_limit_bytes=40 * 1024 * 1024
        ),
    )(*[pltpu.with_memory_space_constraint(operand, pltpu.HBM) for operand in operands])
    return jnp.transpose(mixed)


def solution(mesh):
    in_specs = (
        P(("cfg", "patch"), None),
        P(),
        P(),
        P(None, "head"),
        P(None, "head"),
        P(None, "head"),
        P("head", None),
        P(("cfg", "patch"), "head"),
        P(("cfg", "patch"), "head"),
    )
    return jax.shard_map(
        functools.partial(per_device, mesh.shape["patch"], mesh.shape["head"]),
        mesh=mesh,
        in_specs=in_specs,
        out_specs=P(("cfg", "patch"), "head"),
        check_vma=False,
    )
```

time: 48.1 us -> 47.6 us (0.990)
  the two profiles are of different devices: /device:TPU:6 before, /device:TPU:1 now
where the time goes in v4:
time: 47.6 us; the launch traced here: 47.5 us
  Pallas kernels  46.8 us (98%)
  local copies, waits for them, and re-layouts  0.64 us (1%)
    pallas_call x1, Pallas kernels, per_device(): pl.pallas_call(functools.partial(kernel, n_patch, n_head), out_shape=jax....  46.8 us

profile of v4, /device:TPU:1, one launch (start us, length us, event | category | flops | bytes accessed | tf_op | source)
XLA Modules:
  0.0 47.5 jit_solution(7148937092111335089)
XLA Ops:
  0.0 46.8 %shard_map.91 = bf16[320,128]{1,0:T(8,128)(2,1)S(1)} custom-call(bf16[128,1280]{1,0:T(8,128)(2,1)} %tokens.1, f32[1280]{0:T(1024)} %gain.1, f32[1280]{0:T(1024)} %bias.1, bf16[1280,256]{1,0:T(8,128)(2,1)} %w_query.1, bf16[1280,256]{1,0:T(8,128)(2,1)} %w_key.1, bf16[1280,256]{1,0:T(8,128)(2,1)} %w_value.1, bf16[256,1280]{1,0:T(8,128)(2,1)} %w_out.1, ...), custom_call_target="tpu_custom_call" | custom-call | tf_op jit(solution)/shard_map/pallas_call | solution.py:547
  46.8 0.6 %copy.11 = bf16[128,320]{0,1:T(8,128)(2,1)} copy(bf16[128,320]{0,1:T(8,128)(2,1)S(1)} %bitcast.1) | data formatting | bytes 163840
